TPU v7x, 128 devices: a whole 4x4x4 slice. The times are simulated.
128 devices in a mesh: row: 8 (over y_lo, z), col: 16 (over x, y_hi, core).
Axes of the slice: x: 4, y: 4 (y_hi: 2, y_lo: 2; y = y_hi * 2 + y_lo), z: 4, core: 2. Of those that a mesh axis runs over, the one named last changes fastest.
Arguments:
- hessian: float32 [16384, 8, 16, 128], P('row', None, 'col'), may hold values from -1 to 16, as said below
- weights: bfloat16 [512, 16384], P('col', 'row'), may hold values from -6 to 6
- codes: int32 [512, 8192], P('col', 'row'), may hold values from 0 to 255
- tile_map: int32 [32, 64], P('col', 'row'), may hold values from 0 to 511
- codebooks: float32 [512, 2, 256], replicated, may hold values from -6 to 6
Outputs:
- adjusted_codebooks: float32 [512, 2, 256], replicated
Inputs may be any that keep to these rules, and one draw needn't show every extreme that they name: `hessian`: H is symmetric with a dominant positive diagonal.
All inputs are finite; a program needn't handle non-finite values.
Results may differ from a plain program's by a relative error of at most 0.0003.
Values sent between devices are 32-bit elements; how exact they have to be, the bound alone decides.
No kernel may reach another device: no remote copies, remote signals or barrier semaphores. Data moves between devices by JAX's collectives and lax.ppermute only.
A program may use at most 64 MiB of HBM per device.

v0:
```python
import jax
import jax.numpy as jnp
from jax import lax
from jax.experimental import pallas as pl
from jax.experimental.pallas import tpu as pltpu
from jax.sharding import PartitionSpec as P

F32 = jnp.float32
BF16 = jnp.bfloat16
I32 = jnp.int32
LEARN_RATE = 0.01
BOTH = ("row", "col")
VMEM_LIMIT = 56 * 1024 * 1024
STEP_FLOPS = 18 * 10**9
SORT_FLOPS = 5 * 10**9
SPLIT_FLOPS = 9 * 10**9


def partners(dx, dyh, dcore, dyl, dz):
    flip_col = dx * 4 + dyh * 2 + dcore
    flip_row = dyl * 4 + dz
    return [(i, i ^ (flip_row * 16 + flip_col)) for i in range(128)]


def swap(v, dx=0, dyh=0, dcore=0, dyl=0, dz=0):
    return lax.ppermute(v, BOTH, partners(dx, dyh, dcore, dyl, dz))


def lanes(x, index):
    return jnp.take_along_axis(x, index, axis=1, mode="promise_in_bounds")


def iota(shape, dim):
    return lax.broadcasted_iota(I32, shape, dim)


def split(x):
    high = x.astype(BF16)
    low = (x - high.astype(F32)).astype(BF16)
    return high, low


def dot_nt(a, b):
    return lax.dot_general(a, b, (((1,), (1,)), ((), ())), preferred_element_type=F32)


def dot_nn(a, b):
    return lax.dot_general(a, b, (((1,), (0,)), ((), ())), preferred_element_type=F32)


def whole(x):
    return pl.BlockSpec(x.shape, lambda *_: (0,) * x.ndim)


def in_vmem(n):
    return [pl.BlockSpec(memory_space=pltpu.VMEM)] * n


def in_smem():
    return pl.BlockSpec(memory_space=pltpu.SMEM)


def lookup(code, low_table, high_table):
    low = code & 127
    return jnp.where(code >= 128, lanes(high_table, low), lanes(low_table, low))


def part_pairs():
    lane = iota((256, 256), 1)
    return jnp.where(iota((256, 256), 0) == 2 * (lane & 127) + (lane >> 7), 1.0, 0.0).astype(BF16)


def tile_rows(start, tile, parity):
    return pl.ds(start + tile * 16 + parity, 8, stride=2)


def pieces_kernel(tile_ref, codes_ref, piece_ref, own_ref, held_ref):
    lane = iota((8, 128), 1)
    left = lane < 64
    for q in range(8):
        cut = slice(q * 128, q * 128 + 128)
        held_ref[q * 32 : q * 32 + 32, :] = codes_ref[:, cut]
        for t in range(2):
            even = held_ref[tile_rows(q * 32, t, 0), :]
            odd = held_ref[tile_rows(q * 32, t, 1), :]
            own_ref[t * 8 : t * 8 + 8, cut] = even
            own_ref[16 + t * 8 : 24 + t * 8, cut] = odd
            pair = [
                jnp.where(left, even, pltpu.roll(odd, 64, 1)),
                jnp.where(left, pltpu.roll(even, 64, 1), odd),
            ]
            for h in range(2):
                piece_ref[2 * q + h, t * 8 : t * 8 + 8, :] = pair[h]
        books = jnp.where((lane & 1) == 0, tile_ref[0, q], tile_ref[1, q])
        for h in range(2):
            piece_ref[2 * q + h, 16:24, :] = books


def make_pieces(codes, tile_map):
    return pl.pallas_call(
        pieces_kernel,
        out_shape=[jax.ShapeDtypeStruct((16, 24, 128), I32), jax.ShapeDtypeStruct((32, 1024), I32)],
        in_specs=[in_smem()] + in_vmem(1),
        out_specs=in_vmem(2),
        scratch_shapes=[pltpu.VMEM((256, 128), I32)],
    )(tile_map, codes)


def first_kernel(tile_ref, weights_ref, own_ref, books_ref, out_ref, weight_ref):
    parting = part_pairs()
    for q in range(8):
        parted = dot_nn(weights_ref[:, q * 256 : q * 256 + 256], parting)
        weight_ref[q * 64 : q * 64 + 32, :] = parted[:, 0:128]
        weight_ref[q * 64 + 32 : q * 64 + 64, :] = parted[:, 128:256]
    for q in range(8):
        for t in range(2):
            book = books_ref[tile_ref[t, q]]
            for c in range(2):
                tables = [jnp.broadcast_to(book[c : c + 1, k * 128 : k * 128 + 128], (8, 128)) for k in range(2)]
                for parity in range(2):
                    row = parity * 16 + t * 8
                    code = own_ref[row : row + 8, q * 128 : q * 128 + 128]
                    weight = weight_ref[tile_rows((q * 2 + c) * 32, t, parity), :]
                    out_ref[q, c * 32 + row : c * 32 + row + 8, :] = lookup(code, *tables) - weight
        out_ref[q, 64:96, :] = own_ref[:, q * 128 : q * 128 + 128].astype(F32)
        out_ref[q, 96:104, :] = jnp.where(iota((8, 128), 0) == 0, tile_ref[0, q], tile_ref[1, q]).astype(F32)


def first(weights, own, tile_map, codebooks):
    return pl.pallas_call(
        first_kernel,
        out_shape=jax.ShapeDtypeStruct((8, 104, 128), F32),
        in_specs=[in_smem()] + in_vmem(3),
        out_specs=in_vmem(1)[0],
        scratch_shapes=[pltpu.VMEM((512, 128), F32)],
    )(tile_map, weights, own, codebooks)


def spot(position):
    return ((position & 15) << 3) | (position >> 4)


def spot_back(lane):
    return ((lane & 7) << 4) | (lane >> 3)


def sort_block(keys):
    rows = [keys[v * 8 : v * 8 + 8, :] for v in range(16)]
    sub = iota((8, 128), 0)
    k = 2
    while k <= 128:
        j = k // 2
        while j >= 1:
            if j < 16:
                for v in range(16):
                    if v & j:
                        continue
                    a, b = rows[v], rows[v | j]
                    small, large = jnp.minimum(a, b), jnp.maximum(a, b)
                    if k < 16:
                        rising = (v & k) == 0
                        rows[v], rows[v | j] = (small, large) if rising else (large, small)
                    elif k == 128:
                        rows[v], rows[v | j] = small, large
                    else:
                        up = (sub & (k >> 4)) == 0
                        rows[v], rows[v | j] = jnp.where(up, small, large), jnp.where(up, large, small)
            else:
                step = j >> 4
                lower = (sub & step) == 0
                up = lower if k == 128 else ((sub & (k >> 4)) == 0) == lower
                for v in range(16):
                    other = jnp.where(lower, pltpu.roll(rows[v], 8 - step, 0), pltpu.roll(rows[v], step, 0))
                    rows[v] = jnp.where(up, jnp.minimum(rows[v], other), jnp.maximum(rows[v], other))
            j //= 2
        k *= 2
    return jnp.concatenate(rows, axis=0)


def sort_body(first_kz, *refs):
    lane = iota((256, 128), 1)
    spot32 = iota((8, 128), 1) >> 1
    for n, (piece_ref, packed_ref) in enumerate(zip(refs[: len(refs) // 2], refs[len(refs) // 2 :])):
        base = ((first_kz + n) % 2) * 32 + pl.program_id(0) * 16
        books = jnp.zeros((8, 128), I32)
        for origin in range(16):
            books = jnp.where(spot32 == base + origin, piece_ref[0, origin, 16:24, :], books)
        packed_ref[0, 256:264, :] = books
        key = (piece_ref[0, :, 0:16, :].reshape(256, 128) * 128 + lane).astype(F32)
        halves = [sort_block(key[h * 128 : h * 128 + 128, :].T).T for h in range(2)]
        code = jnp.concatenate(halves, axis=0).astype(I32)
        counts = []
        for half in range(2):
            limit = (half * 128 + lane + 1) * 128
            count = jnp.zeros((256, 128), I32)
            for step in (64, 32, 16, 8, 4, 2, 1, 1):
                below = lanes(code, spot(count + (step - 1))) < limit
                count = jnp.where(below, count + step, count)
            counts.append(count)
        packed_ref[0, 0:256, :] = (code & 127) | (counts[0] << 8) | (counts[1] << 16)


def sort_codes(pieces, first_kz):
    many = len(pieces)

    def sort_kernel(*refs):
        sort_body(first_kz, *refs)

    return pl.pallas_call(
        sort_kernel,
        out_shape=[jax.ShapeDtypeStruct((2, 264, 128), I32)] * many,
        grid=(2,),
        in_specs=[pl.BlockSpec((1, 16, 24, 128), lambda j: (j, 0, 0, 0))] * many,
        out_specs=[pl.BlockSpec((1, 264, 128), lambda j: (j, 0, 0))] * many,
        compiler_params=pltpu.CompilerParams(vmem_limit_bytes=VMEM_LIMIT),
        cost_estimate=pl.CostEstimate(flops=many * SORT_FLOPS, bytes_accessed=many * 1024 * 1024, transcendentals=0),
    )(*pieces)


def split_kernel(where_ref, hessian_ref, right_ref):
    for j in range(8):
        for c in range(2):
            high, low = split(hessian_ref[pl.ds(c * 8 + j, 128, stride=16), :])
            cut = slice(j * 128, j * 128 + 128)
            right_ref[0, c * 128 : c * 128 + 128, cut] = high
            right_ref[0, 256 + c * 128 : 256 + c * 128 + 128, cut] = low


def split_hessian(where, rows):
    return pl.pallas_call(
        split_kernel,
        out_shape=jax.ShapeDtypeStruct((8, 512, 1024), BF16),
        grid=(8,),
        in_specs=[in_smem(), pl.BlockSpec((2048, 128), lambda q: (q, 0))],
        out_specs=pl.BlockSpec((1, 512, 1024), lambda q: (q, 0, 0)),
        compiler_params=pltpu.CompilerParams(vmem_limit_bytes=VMEM_LIMIT),
        cost_estimate=pl.CostEstimate(flops=SPLIT_FLOPS, bytes_accessed=20 * 1024 * 1024, transcendentals=0),
    )(where, rows)


def step_body(second, where_ref, packed_refs, rights, refs):
    error_refs, refs = (refs[:8], refs[8:16]), refs[16:]
    if second:
        (near_ref, far_ref, book_col_ref), refs = refs[:3], refs[3:]
    keep_ref, send_ref, left0_ref, left1_ref, grad_ref, sums_ref, table_ref = refs
    n = pl.program_id(0)
    row, col, place = where_ref[0], where_ref[1], where_ref[2]

    def multiply(left_ref, right_ref):
        for part in range(4):
            for m in range(2):
                rows = slice(m * 256, m * 256 + 256)
                cut = slice(part * 256, part * 256 + 256)
                more = dot_nn(left_ref[rows, 0:512], right_ref[0, :, cut]) + dot_nn(left_ref[rows, 512:768], right_ref[0, 0:256, cut])
                grad_ref[2 * part, rows, :] += more[:, 0:128]
                grad_ref[2 * part + 1, rows, :] += more[:, 128:256]

    def prepare(half, left_ref):
        b = jnp.minimum(2 * n + half, 7)
        for core in range(2):
            for kx in range(4):
                which = core * 4 + kx
                for kyh in range(2):
                    start = pl.multiple_of((col ^ (kx * 4 + kyh * 2 + core)) * 16, 16)
                    base = core * 16 + (kx * 2 + kyh) * 2
                    for c in range(2):
                        if second:
                            tables = [
                                [
                                    jnp.broadcast_to(table_ref[b, base + t : base + t + 1, (c * 2 + k) * 128 : (c * 2 + k) * 128 + 128], (8, 128))
                                    for k in range(2)
                                ]
                                for t in range(2)
                            ]
                        for parity in range(2):
                            row = c * 32 + parity * 16
                            value = error_refs[half][which][kyh, 0, row : row + 16, :]
                            if second:
                                row = 64 + parity * 16
                                code = error_refs[half][which][kyh, 0, row : row + 16, :].astype(I32)
                                moves = [lookup(code[t * 8 : t * 8 + 8], *tables[t]) for t in range(2)]
                                value = value - jnp.concatenate(moves, axis=0)
                            high, low = split(value)
                            rows = pl.ds(parity * 256 + start, 16)
                            left_ref[rows, c * 128 : c * 128 + 128] = high
                            left_ref[rows, 256 + c * 128 : 256 + c * 128 + 128] = high
                            left_ref[rows, 512 + c * 128 : 512 + c * 128 + 128] = low

    @pl.when(n == 0)
    def _():
        left1_ref[...] = jnp.zeros((512, 768), BF16)
        grad_ref[...] = jnp.zeros((8, 512, 128), F32)
        if second:
            chosen = jnp.where((book_col_ref[...] ^ place) == iota((256, 512), 1), 1.0, 0.0).astype(BF16)
            total = jnp.zeros((256, 512), F32)
            for part, ref in ((0, near_ref), (1, far_ref)):
                high, low = split(ref[...])
                here = chosen[:, part * 256 : part * 256 + 256]
                total = total + dot_nn(here, high) + dot_nn(here, low)
            table_ref[...] = (total * LEARN_RATE).reshape(8, 32, 512)

    prepare(0, left0_ref)
    multiply(left1_ref, rights[0])

    @pl.when(n < 4)
    def _():
        prepare(1, left1_ref)
        multiply(left0_ref, rights[1])

    @pl.when(n == 4)
    def _():
        parting = part_pairs()
        running = jnp.where(spot_back(iota((256, 128), 0) & 127) <= iota((256, 128), 1), 1.0, 0.0).astype(BF16)
        lane = iota((32, 128), 1)
        for kz in range(4):
            for dyl in range(2):
                j = row ^ (dyl * 4 + kz)
                at = kz * 2 + dyl
                both = jnp.concatenate([grad_ref[j, 0:256, :], grad_ref[j, 256:512, :]], axis=1)
                high, low = split(both)
                pairs = dot_nn(high, parting) + dot_nn(low, parting)
                packed = packed_refs[kz][dyl, 0:256, :]
                source = packed & 127
                counts = [(packed >> 8) & 255, packed >> 16]
                for c in range(2):
                    ordered = lanes(pairs[:, c * 128 : c * 128 + 128], source)
                    prefix = dot_nn(jnp.concatenate(split(ordered), axis=1), running)
                    upto = []
                    for count in counts:
                        value = jnp.where(count > 0, lanes(prefix, jnp.maximum(count - 1, 0)), 0.0)
                        upto.append(value.reshape(32, 8, 128).sum(axis=1))
                    earlier = [pltpu.roll(v, 1, 1) for v in upto]
                    low_sums = 2.0 * (upto[0] - jnp.where(lane == 0, 0.0, earlier[0]))
                    high_sums = 2.0 * (upto[1] - jnp.where(lane == 0, earlier[0], earlier[1]))
                    sums_ref[at, :, c * 256 : c * 256 + 128] = low_sums
                    sums_ref[at, :, c * 256 + 128 : c * 256 + 256] = high_sums
        books = [packed_refs[kz][0, 256:257, :] + packed_refs[kz][1, 256:257, :] for kz in range(4)]
        books = jnp.concatenate([books[0] + books[1], books[2] + books[3]], axis=1)
        chosen = jnp.where((iota((512, 256), 0) ^ place) == books, 1.0, 0.0).astype(BF16)
        high, low = split(sums_ref[...].reshape(256, 512))
        total = dot_nn(chosen, high) + dot_nn(chosen, low)
        keep_ref[...] = total[0:256]
        send_ref[...] = total[256:512]


def step(second, place, packed, right, errors, rest):
    def kernel(where_ref, *refs):
        step_body(second, where_ref, refs[0:4], refs[4:6], refs[6:])

    def tile_column(half):
        return lambda n: jnp.clip(2 * n + half, 0, 7)

    right_specs, error_specs = [], []
    height = 104 if second else 64
    for half in (-1, 0):
        right_specs.append(pl.BlockSpec((1, 512, 1024), lambda n, f=tile_column(half): (f(n), 0, 0)))
    for half in (0, 1):
        error_specs += [pl.BlockSpec((2, 1, height, 128), lambda n, f=tile_column(half): (0, f(n), 0, 0))] * 8
    half = jax.ShapeDtypeStruct((256, 512), F32)
    return pl.pallas_call(
        kernel,
        out_shape=[half, half],
        grid=(5,),
        in_specs=[in_smem()]
        + [whole(x) for x in packed]
        + right_specs
        + error_specs
        + [whole(x) for x in rest],
        out_specs=[pl.BlockSpec((256, 512), lambda n: (0, 0))] * 2,
        scratch_shapes=[
            pltpu.VMEM((512, 768), BF16),
            pltpu.VMEM((512, 768), BF16),
            pltpu.VMEM((8, 512, 128), F32),
            pltpu.VMEM((8, 32, 512), F32),
            pltpu.VMEM((8, 32, 512), F32),
        ],
        compiler_params=pltpu.CompilerParams(vmem_limit_bytes=VMEM_LIMIT),
        cost_estimate=pl.CostEstimate(flops=STEP_FLOPS, bytes_accessed=16 * 1024 * 1024, transcendentals=0),
    )(place, *packed, right, right, *errors, *errors, *rest)


def update_kernel(where_ref, books_ref, near_ref, far_ref, out_ref):
    for part, ref in enumerate((near_ref, far_ref)):
        for k in range(4):
            start = pl.multiple_of((part * 256 + k * 64) ^ where_ref[2], 64)
            for c in range(2):
                moved = LEARN_RATE * ref[k * 64 : k * 64 + 64, c * 256 : c * 256 + 256]
                out_ref[pl.ds(start, 64), c, :] = books_ref[pl.ds(start, 64), c, :] - moved


def update(where, codebooks, near, far):
    return pl.pallas_call(
        update_kernel,
        out_shape=jax.ShapeDtypeStruct((512, 2, 256), F32),
        in_specs=[in_smem()] + in_vmem(3),
        out_specs=in_vmem(1)[0],
    )(where, codebooks, near, far)


def sum_all(keep, send, beside):
    half = keep + swap(send, dcore=1)
    quarter = [half[k * 64 : k * 64 + 64] for k in range(4)]
    got = [None] + [swap(quarter[k], dx=k) for k in (1, 2, 3)]
    s = (quarter[0] + got[2]) + (got[1] + got[3])
    s, beside = hold(s, beside)
    got = [None] + [swap(s, dyl=k & 1, dyh=k >> 1) for k in (1, 2, 3)]
    s = (s + got[2]) + (got[1] + got[3])
    got = [None] + [swap(s, dz=k) for k in (1, 2, 3)]
    s = (s + got[2]) + (got[1] + got[3])
    near = jnp.concatenate([s] + [swap(s, dx=k) for k in (1, 2, 3)])
    return near, swap(near, dcore=1), beside


def hold(*values):
    return lax.optimization_barrier(values)


def pair_up(own):
    return jnp.stack([own, swap(own, dyh=1)])


def over_x(pair):
    return [pair] + [swap(pair, dx=k) for k in (1, 2, 3)]


def both_cores(near):
    return list(near) + [swap(v, dcore=1) for v in near]


def per_device(hessian, weights, codes, tile_map, codebooks):
    row, col = lax.axis_index("row").astype(I32), lax.axis_index("col").astype(I32)
    where = jnp.stack([row, col, (col & 1) * 256 + (col >> 2) * 64])
    pieces, own = make_pieces(codes, tile_map)
    pieces = lax.all_to_all(pieces, "col", 0, 0, tiled=True)
    pair = pair_up(first(weights, own, tile_map, codebooks))
    pieces, pair = hold(pieces, pair)

    around = over_x(pair)
    pieces = jnp.stack([pieces, swap(pieces, dyl=1)])
    pieces, later = hold(pieces, where)
    right = split_hessian(later, hessian.reshape(16384, 128))
    packed = sort_codes([pieces], 0)
    right, packed, one, three = hold(right, packed, *[swap(pieces, dz=k) for k in (1, 3)])
    pieces, one = hold(pieces, one)
    two = swap(pieces, dz=2)
    packed_one, packed_three = sort_codes([one], 1), sort_codes([three], 3)
    packed_one, packed_three, *around = hold(packed_one, packed_three, *around)
    around = both_cores(around)
    packed = [*packed, *packed_one, *sort_codes([two], 2), *packed_three]
    keep, send = step(False, where, packed, right, around, [])
    book_col = jnp.concatenate([v[:, :, 96:98, 0] for v in around])
    book_col = book_col.transpose(1, 0, 2).reshape(256, 1).astype(I32)
    near, far, book_col = sum_all(keep, send, book_col)
    keep, send = step(True, where, packed, right, around, [near, far, book_col])
    near, far, codebooks = sum_all(keep, send, update(where, codebooks, near, far))
    return update(where, codebooks, near, far)


def solution(mesh):
    placed = (P("row", None, "col", None), P("col", "row"), P("col", "row"), P("col", "row"), P())
    return jax.shard_map(per_device, mesh=mesh, in_specs=placed, out_specs=P(), check_vma=False)
```

profile of v0, /device:TPU:1, one launch (start us, length us, event | category | flops | bytes accessed | tf_op | source)
XLA Modules:
  0.0 218.8 jit_solution(16119639666122632672)
XLA Ops:
  1.7 2.6 %shard_map.56 = f32[8,104,128]{2,1,0:T(8,128)} custom-call(s32[2,8]{1,0:T(2,128)} %tile_ref.3, bf16[32,2048]{1,0:T(8,128)(2,1)} %weights_ref.1, s32[32,1024]{1,0:T(8,128)} %get-tuple-element.32.own_ref, f32[512,2,256]{2,1,0:T(2,128)} %books_ref.3), custom_call_target="tpu_custom_call" | custom-call | tf_op jit(solution)/shard_map/pallas_call | solution.py:130
  4.3 3.7 %collective-permute-start = (f32[8,104,128]{2,1,0:T(8,128)}, f32[8,104,128]{2,1,0:T(8,128)S(1)}, u32[]{:S(2)}, u32[]{:S(2)}) collective-permute-start(f32[8,104,128]{2,1,0:T(8,128)} %shard_map.56), channel_id=1, source_target_pairs={{0,2},{1,3},{2,0},{3,1},{4,6},{5,7},{6,4},{7,5},{8,10},{9,11},{10,... | collective-permute-start | bytes 1277960 | tf_op jit(solution)/shard_map/ppermute | solution.py:26
  8.0 5.3 %all-to-all-start = ((s32[16,24,128]{2,1,0:T(8,128)}), s32[16,24,128]{2,1,0:T(8,128)S(1)}, u32[]{:S(2)}, u32[]{:S(2)}) async-start(s32[16,24,128]{2,1,0:T(8,128)} %get-tuple-element.31), calls=%async_computation | async-start | bytes 393216 | tf_op jit(solution)/shard_map/all_to_all | solution.py:434
  13.3 4.2 %collective-permute-done = f32[8,104,128]{2,1,0:T(8,128)S(1)} collective-permute-done((f32[8,104,128]{2,1,0:T(8,128)}, f32[8,104,128]{2,1,0:T(8,128)S(1)}, u32[]{:S(2)}, u32[]{:S(2)}) %collective-permute-start) | collective-permute-done | bytes 426016 | tf_op jit(solution)/shard_map/ppermute | solution.py:26
  18.6 3.0 %all-to-all-done = s32[16,24,128]{2,1,0:T(8,128)S(1)} async-done(((s32[16,24,128]{2,1,0:T(8,128)}), s32[16,24,128]{2,1,0:T(8,128)S(1)}, u32[]{:S(2)}, u32[]{:S(2)}) %all-to-all-start) | async-done | bytes 196640 | tf_op jit(solution)/shard_map/all_to_all | solution.py:434
  27.7 3.8 %collective-permute-start.3 = (s32[2,16,24,128]{3,2,1,0:T(8,128)S(1)}, s32[2,16,24,128]{3,2,1,0:T(8,128)S(1)}, u32[]{:S(2)}, u32[]{:S(2)}) collective-permute-start(s32[2,16,24,128]{3,2,1,0:T(8,128)S(1)} %pad_add_fusion.refs_0_), channel_id=1, source_target_pairs={{0,48},{1,49},{2,50},{3,51},{4,52},{5,53},{6,54},{7,55},{8,56},{9,... | collective-permute-start | bytes 1179656 | tf_op jit(solution)/shard_map/ppermute | solution.py:26
  31.5 10.5 %shard_map.57.refs_4_.refs_5_ = bf16[8,512,1024]{2,1,0:T(8,128)(2,1)} custom-call(s32[3]{0:T(128)} %pad_add_fusion.1.where_ref, f32[16384,128]{1,0:T(8,128)} %bitcast.30), custom_call_target="tpu_custom_call" | custom-call | flops 8999999488 | bytes 20971520 | tf_op jit(solution)/shard_map/pallas_call | solution.py:230
  42.0 5.3 %shard_map.58.refs_0_ = s32[2,264,128]{2,1,0:T(8,128)} custom-call(s32[2,16,24,128]{3,2,1,0:T(8,128)} %copy-done.5), custom_call_target="tpu_custom_call" | custom-call | flops 5000000000 | bytes 1048576 | tf_op jit(solution)/shard_map/pallas_call | solution.py:209
  48.7 5.3 %shard_map.59.refs_1_ = s32[2,264,128]{2,1,0:T(8,128)} custom-call(s32[2,16,24,128]{3,2,1,0:T(8,128)} %copy-done.10), custom_call_target="tpu_custom_call" | custom-call | flops 5000000000 | bytes 1048576 | tf_op jit(solution)/shard_map/pallas_call | solution.py:209
  54.0 5.3 %shard_map.60.refs_3_ = s32[2,264,128]{2,1,0:T(8,128)} custom-call(s32[2,16,24,128]{3,2,1,0:T(8,128)} %copy-done.9), custom_call_target="tpu_custom_call" | custom-call | flops 5000000000 | bytes 1048576 | tf_op jit(solution)/shard_map/pallas_call | solution.py:209
  59.3 3.3 %collective-permute-done.6.refs_9_.refs_17_ = f32[2,8,104,128]{3,2,1,0:T(8,128)S(1)} collective-permute-done((f32[2,8,104,128]{3,2,1,0:T(8,128)S(1)}, f32[2,8,104,128]{3,2,1,0:T(8,128)S(1)}, u32[]{:S(2)}, u32[]{:S(2)}) %collective-permute-start.6) | collective-permute-done | bytes 852000 | tf_op jit(solution)/shard_map/ppermute | solution.py:26
  67.8 5.3 %shard_map.61.refs_2_ = s32[2,264,128]{2,1,0:T(8,128)} custom-call(s32[2,16,24,128]{3,2,1,0:T(8,128)} %copy-done.8), custom_call_target="tpu_custom_call" | custom-call | flops 5000000000 | bytes 1048576 | tf_op jit(solution)/shard_map/pallas_call | solution.py:209
  75.1 19.6 %shard_map.62 = (f32[256,512]{1,0:T(8,128)}, f32[256,512]{1,0:T(8,128)}) custom-call(s32[3]{0:T(128)} %pad_add_fusion.1.where_ref, s32[2,264,128]{2,1,0:T(8,128)} %shard_map.58.refs_0_, s32[2,264,128]{2,1,0:T(8,128)} %shard_map.59.refs_1_, s32[2,264,128]{2,1,0:T(8,128)} %shard_map.61.refs_2_, s32[2,264,128]{2,1,0:T(8,128)} %shard_map.60.refs_3_, ...), custom_call_target="tpu_custom_call" | custom-call | flops 17999998976 | bytes 16777216 | tf_op jit(solution)/shard_map/pallas_call | solution.py:360
  104.6 3.4 %collective-permute-done.13 = f32[64,512]{1,0:T(8,128)S(1)} collective-permute-done((f32[64,512]{1,0:T(8,128)S(1)}, f32[64,512]{1,0:T(8,128)S(1)}, u32[]{:S(2)}, u32[]{:S(2)}) %collective-permute-start.13) | collective-permute-done | bytes 131104 | tf_op jit(solution)/shard_map/ppermute | solution.py:26
  113.2 3.3 %collective-permute-done.16 = f32[64,512]{1,0:T(8,128)S(1)} collective-permute-done((f32[64,512]{1,0:T(8,128)S(1)}, f32[64,512]{1,0:T(8,128)S(1)}, u32[]{:S(2)}, u32[]{:S(2)}) %collective-permute-start.16) | collective-permute-done | bytes 131104 | tf_op jit(solution)/shard_map/ppermute | solution.py:26
  116.6 3.8 %collective-permute-start.21 = (f32[64,512]{1,0:T(8,128)S(1)}, f32[64,512]{1,0:T(8,128)S(1)}, u32[]{:S(2)}, u32[]{:S(2)}) collective-permute-start(f32[64,512]{1,0:T(8,128)S(1)} %add_add_fusion.3), channel_id=1, source_target_pairs={{0,48},{1,49},{2,50},{3,51},{4,52},{5,53},{6,54},{7,55},{8,56},{9,... | collective-permute-start | bytes 393224 | tf_op jit(solution)/shard_map/ppermute | solution.py:26
  120.4 11.3 %collective-permute-start.19 = (f32[64,512]{1,0:T(8,128)S(1)}, f32[64,512]{1,0:T(8,128)S(1)}, u32[]{:S(2)}, u32[]{:S(2)}) collective-permute-start(f32[64,512]{1,0:T(8,128)S(1)} %add_add_fusion.3), channel_id=1, source_target_pairs={{0,32},{1,33},{2,34},{3,35},{4,36},{5,37},{6,38},{7,39},{8,40},{9,... | collective-permute-start | bytes 393224 | tf_op jit(solution)/shard_map/ppermute | solution.py:26
  131.7 4.0 %collective-permute-done.19 = f32[64,512]{1,0:T(8,128)S(1)} collective-permute-done((f32[64,512]{1,0:T(8,128)S(1)}, f32[64,512]{1,0:T(8,128)S(1)}, u32[]{:S(2)}, u32[]{:S(2)}) %collective-permute-start.19) | collective-permute-done | bytes 131104 | tf_op jit(solution)/shard_map/ppermute | solution.py:26
  143.0 5.7 %collective-permute-start.25 = (f32[256,512]{1,0:T(8,128)S(1)}, f32[256,512]{1,0:T(8,128)S(1)}, u32[]{:S(2)}, u32[]{:S(2)}) collective-permute-start(f32[256,512]{1,0:T(8,128)S(1)} %pad_maximum_fusion.1.refs_22_.near_ref), channel_id=1, source_target_pairs={{0,1},{1,0},{2,3},{3,2},{4,5},{5,4},{6,7},{7,6},{8,9},{9,8},{10,11... | collective-permute-start | bytes 1572872 | tf_op jit(solution)/shard_map/ppermute | solution.py:26
  151.0 19.9 %shard_map.63 = (f32[256,512]{1,0:T(8,128)}, f32[256,512]{1,0:T(8,128)}) custom-call(s32[3]{0:T(128)} %pad_add_fusion.1.where_ref, s32[2,264,128]{2,1,0:T(8,128)} %shard_map.58.refs_0_, s32[2,264,128]{2,1,0:T(8,128)} %shard_map.59.refs_1_, s32[2,264,128]{2,1,0:T(8,128)} %shard_map.61.refs_2_, s32[2,264,128]{2,1,0:T(8,128)} %shard_map.60.refs_3_, ...), custom_call_target="tpu_custom_call" | custom-call | flops 17999998976 | bytes 16777216 | tf_op jit(solution)/shard_map/pallas_call | solution.py:360
  178.3 3.2 %shard_map.64.books_ref = f32[512,2,256]{2,1,0:T(2,128)} custom-call(s32[3]{0:T(128)} %pad_add_fusion.1.where_ref, f32[512,2,256]{2,1,0:T(2,128)} %books_ref.3, f32[256,512]{1,0:T(8,128)} %copy-done, f32[256,512]{1,0:T(8,128)} %copy-done.3), custom_call_target="tpu_custom_call" | custom-call | tf_op jit(solution)/shard_map/pallas_call | solution.py:392
  197.4 2.6 %collective-permute-done.33 = f32[64,512]{1,0:T(8,128)S(1)} collective-permute-done((f32[64,512]{1,0:T(8,128)S(1)}, f32[64,512]{1,0:T(8,128)S(1)}, u32[]{:S(2)}, u32[]{:S(2)}) %collective-permute-start.33) | collective-permute-done | bytes 131104 | tf_op jit(solution)/shard_map/ppermute | solution.py:26
  207.3 5.9 %collective-permute-start.39 = (f32[256,512]{1,0:T(8,128)S(1)}, f32[256,512]{1,0:T(8,128)S(1)}, u32[]{:S(2)}, u32[]{:S(2)}) collective-permute-start(f32[256,512]{1,0:T(8,128)S(1)} %pad_maximum_fusion.2.near_ref), channel_id=1, source_target_pairs={{0,1},{1,0},{2,3},{3,2},{4,5},{5,4},{6,7},{7,6},{8,9},{9,8},{10,11... | collective-permute-start | bytes 1572872 | tf_op jit(solution)/shard_map/ppermute | solution.py:26
  215.5 3.2 %shard_map.65 = f32[512,2,256]{2,1,0:T(2,128)} custom-call(s32[3]{0:T(128)} %pad_add_fusion.1.where_ref, f32[512,2,256]{2,1,0:T(2,128)} %shard_map.64.books_ref, f32[256,512]{1,0:T(8,128)} %copy-done.1, f32[256,512]{1,0:T(8,128)} %copy-done.4), custom_call_target="tpu_custom_call" | custom-call | tf_op jit(solution)/shard_map/pallas_call | solution.py:392
  (134 shorter events, 74.9 us)
Async XLA Ops:
  4.3 13.2 %collective-permute-start = (f32[8,104,128]{2,1,0:T(8,128)}, f32[8,104,128]{2,1,0:T(8,128)S(1)}, u32[]{:S(2)}, u32[]{:S(2)}) collective-permute-start(f32[8,104,128]{2,1,0:T(8,128)} %shard_map.56), channel_id=1, source_target_pairs={{0,2},{1,3},{2,0},{3,1},{4,6},{5,7},{6,4},{7,5},{8,10},{9,11},{10,... | collective-permute-start | bytes 1277960 | tf_op jit(solution)/shard_map/ppermute | solution.py:26
  8.0 13.6 %all-to-all-start = ((s32[16,24,128]{2,1,0:T(8,128)}), s32[16,24,128]{2,1,0:T(8,128)S(1)}, u32[]{:S(2)}, u32[]{:S(2)}) async-start(s32[16,24,128]{2,1,0:T(8,128)} %get-tuple-element.31), calls=%async_computation | async-start | bytes 393216 | tf_op jit(solution)/shard_map/all_to_all | solution.py:434
  21.6 6.1 %collective-permute-start.1 = (s32[16,24,128]{2,1,0:T(8,128)S(1)}, s32[16,24,128]{2,1,0:T(8,128)S(1)}, u32[]{:S(2)}, u32[]{:S(2)}) collective-permute-start(s32[16,24,128]{2,1,0:T(8,128)S(1)} %all-to-all-done), channel_id=1, source_target_pairs={{0,64},{1,65},{2,66},{3,67},{4,68},{5,69},{6,70},{7,71},{8,72},{9,... | collective-permute-start | bytes 589832 | tf_op jit(solution)/shard_map/ppermute | solution.py:26
  23.3 39.3 %collective-permute-start.6 = (f32[2,8,104,128]{3,2,1,0:T(8,128)S(1)}, f32[2,8,104,128]{3,2,1,0:T(8,128)S(1)}, u32[]{:S(2)}, u32[]{:S(2)}) collective-permute-start(f32[2,8,104,128]{3,2,1,0:T(8,128)S(1)} %pad_maximum_fusion.refs_6_.refs_14_), channel_id=1, source_target_pairs={{0,12},{1,13},{2,14},{3,15},{4,8},{5,9},{6,10},{7,11},{8,4},{9,5},... | collective-permute-start | bytes 2555912 | tf_op jit(solution)/shard_map/ppermute | solution.py:26
  25.0 37.5 %collective-permute-start.5 = (f32[2,8,104,128]{3,2,1,0:T(8,128)S(1)}, f32[2,8,104,128]{3,2,1,0:T(8,128)S(1)}, u32[]{:S(2)}, u32[]{:S(2)}) collective-permute-start(f32[2,8,104,128]{3,2,1,0:T(8,128)S(1)} %pad_maximum_fusion.refs_6_.refs_14_), channel_id=1, source_target_pairs={{0,8},{1,9},{2,10},{3,11},{4,12},{5,13},{6,14},{7,15},{8,0},{9,1},... | collective-permute-start | bytes 2555912 | tf_op jit(solution)/shard_map/ppermute | solution.py:26
  25.5 37.4 %collective-permute-start.4 = (f32[2,8,104,128]{3,2,1,0:T(8,128)S(1)}, f32[2,8,104,128]{3,2,1,0:T(8,128)}, u32[]{:S(2)}, u32[]{:S(2)}) collective-permute-start(f32[2,8,104,128]{3,2,1,0:T(8,128)S(1)} %pad_maximum_fusion.refs_6_.refs_14_), channel_id=1, source_target_pairs={{0,4},{1,5},{2,6},{3,7},{4,0},{5,1},{6,2},{7,3},{8,12},{9,13},{10,... | collective-permute-start | bytes 2555912 | tf_op jit(solution)/shard_map/ppermute | solution.py:26
  27.7 19.6 %collective-permute-start.3 = (s32[2,16,24,128]{3,2,1,0:T(8,128)S(1)}, s32[2,16,24,128]{3,2,1,0:T(8,128)S(1)}, u32[]{:S(2)}, u32[]{:S(2)}) collective-permute-start(s32[2,16,24,128]{3,2,1,0:T(8,128)S(1)} %pad_add_fusion.refs_0_), channel_id=1, source_target_pairs={{0,48},{1,49},{2,50},{3,51},{4,52},{5,53},{6,54},{7,55},{8,56},{9,... | collective-permute-start | bytes 1179656 | tf_op jit(solution)/shard_map/ppermute | solution.py:26
  31.5 15.8 %collective-permute-start.2 = (s32[2,16,24,128]{3,2,1,0:T(8,128)S(1)}, s32[2,16,24,128]{3,2,1,0:T(8,128)S(1)}, u32[]{:S(2)}, u32[]{:S(2)}) collective-permute-start(s32[2,16,24,128]{3,2,1,0:T(8,128)S(1)} %pad_add_fusion.refs_0_), channel_id=1, source_target_pairs={{0,16},{1,17},{2,18},{3,19},{4,20},{5,21},{6,22},{7,23},{8,24},{9,... | collective-permute-start | bytes 1179656 | tf_op jit(solution)/shard_map/ppermute | solution.py:26
  47.3 19.7 %collective-permute-start.7 = (s32[2,16,24,128]{3,2,1,0:T(8,128)}, s32[2,16,24,128]{3,2,1,0:T(8,128)S(1)}, u32[]{:S(2)}, u32[]{:S(2)}) collective-permute-start(s32[2,16,24,128]{3,2,1,0:T(8,128)} %copy-done.5), channel_id=1, source_target_pairs={{0,32},{1,33},{2,34},{3,35},{4,36},{5,37},{6,38},{7,39},{8,40},{9,... | collective-permute-start | bytes 1179656 | tf_op jit(solution)/shard_map/ppermute | solution.py:26
  63.0 10.1 %collective-permute-start.8 = (f32[2,8,104,128]{3,2,1,0:T(8,128)S(1)}, f32[2,8,104,128]{3,2,1,0:T(8,128)}, u32[]{:S(2)}, u32[]{:S(2)}) collective-permute-start(f32[2,8,104,128]{3,2,1,0:T(8,128)S(1)} %pad_maximum_fusion.refs_6_.refs_14_), channel_id=1, source_target_pairs={{0,1},{1,0},{2,3},{3,2},{4,5},{5,4},{6,7},{7,6},{8,9},{9,8},{10,11... | collective-permute-start | bytes 2555912 | tf_op jit(solution)/shard_map/ppermute | solution.py:26
  65.7 8.3 %collective-permute-start.9 = (f32[2,8,104,128]{3,2,1,0:T(8,128)}, f32[2,8,104,128]{3,2,1,0:T(8,128)}, u32[]{:S(2)}, u32[]{:S(2)}) collective-permute-start(f32[2,8,104,128]{3,2,1,0:T(8,128)} %collective-permute-done.4.refs_7_.refs_15_), channel_id=1, source_target_pairs={{0,1},{1,0},{2,3},{3,2},{4,5},{5,4},{6,7},{7,6},{8,9},{9,8},{10,11... | collective-permute-start | bytes 2555912 | tf_op jit(solution)/shard_map/ppermute | solution.py:26
  65.8 9.3 %collective-permute-start.10 = (f32[2,8,104,128]{3,2,1,0:T(8,128)S(1)}, f32[2,8,104,128]{3,2,1,0:T(8,128)}, u32[]{:S(2)}, u32[]{:S(2)}) collective-permute-start(f32[2,8,104,128]{3,2,1,0:T(8,128)S(1)} %collective-permute-done.5.refs_8_.refs_16_), channel_id=1, source_target_pairs={{0,1},{1,0},{2,3},{3,2},{4,5},{5,4},{6,7},{7,6},{8,9},{9,8},{10,11... | collective-permute-start | bytes 2555912 | tf_op jit(solution)/shard_map/ppermute | solution.py:26
  66.3 8.8 %collective-permute-start.11 = (f32[2,8,104,128]{3,2,1,0:T(8,128)S(1)}, f32[2,8,104,128]{3,2,1,0:T(8,128)}, u32[]{:S(2)}, u32[]{:S(2)}) collective-permute-start(f32[2,8,104,128]{3,2,1,0:T(8,128)S(1)} %collective-permute-done.6.refs_9_.refs_17_), channel_id=1, source_target_pairs={{0,1},{1,0},{2,3},{3,2},{4,5},{5,4},{6,7},{7,6},{8,9},{9,8},{10,11... | collective-permute-start | bytes 2555912 | tf_op jit(solution)/shard_map/ppermute | solution.py:26
  98.2 6.2 %collective-permute-start.15 = (f32[64,512]{1,0:T(8,128)S(1)}, f32[64,512]{1,0:T(8,128)S(1)}, u32[]{:S(2)}, u32[]{:S(2)}) collective-permute-start(f32[64,512]{1,0:T(8,128)S(1)} %get-tuple-element.60), channel_id=1, source_target_pairs={{0,12},{1,13},{2,14},{3,15},{4,8},{5,9},{6,10},{7,11},{8,4},{9,5},... | collective-permute-start | bytes 393224 | tf_op jit(solution)/shard_map/ppermute | solution.py:26
  100.0 8.0 %collective-permute-start.13 = (f32[64,512]{1,0:T(8,128)S(1)}, f32[64,512]{1,0:T(8,128)S(1)}, u32[]{:S(2)}, u32[]{:S(2)}) collective-permute-start(f32[64,512]{1,0:T(8,128)S(1)} %get-tuple-element.62), channel_id=1, source_target_pairs={{0,8},{1,9},{2,10},{3,11},{4,12},{5,13},{6,14},{7,15},{8,0},{9,1},... | collective-permute-start | bytes 393224 | tf_op jit(solution)/shard_map/ppermute | solution.py:26
  109.7 6.9 %collective-permute-start.16 = (f32[64,512]{1,0:T(8,128)S(1)}, f32[64,512]{1,0:T(8,128)S(1)}, u32[]{:S(2)}, u32[]{:S(2)}) collective-permute-start(f32[64,512]{1,0:T(8,128)S(1)} %fusion.1), channel_id=1, source_target_pairs={{0,2},{1,3},{2,0},{3,1},{4,6},{5,7},{6,4},{7,5},{8,10},{9,11},{10,... | collective-permute-start | bytes 393224 | tf_op jit(solution)/shard_map/ppermute | solution.py:26
  116.6 15.1 %collective-permute-start.21 = (f32[64,512]{1,0:T(8,128)S(1)}, f32[64,512]{1,0:T(8,128)S(1)}, u32[]{:S(2)}, u32[]{:S(2)}) collective-permute-start(f32[64,512]{1,0:T(8,128)S(1)} %add_add_fusion.3), channel_id=1, source_target_pairs={{0,48},{1,49},{2,50},{3,51},{4,52},{5,53},{6,54},{7,55},{8,56},{9,... | collective-permute-start | bytes 393224 | tf_op jit(solution)/shard_map/ppermute | solution.py:26
  120.4 11.3 %collective-permute-start.20 = (f32[64,512]{1,0:T(8,128)S(1)}, f32[64,512]{1,0:T(8,128)S(1)}, u32[]{:S(2)}, u32[]{:S(2)}) collective-permute-start(f32[64,512]{1,0:T(8,128)S(1)} %add_add_fusion.3), channel_id=1, source_target_pairs={{0,16},{1,17},{2,18},{3,19},{4,20},{5,21},{6,22},{7,23},{8,24},{9,... | collective-permute-start | bytes 393224 | tf_op jit(solution)/shard_map/ppermute | solution.py:26
  120.4 15.3 %collective-permute-start.19 = (f32[64,512]{1,0:T(8,128)S(1)}, f32[64,512]{1,0:T(8,128)S(1)}, u32[]{:S(2)}, u32[]{:S(2)}) collective-permute-start(f32[64,512]{1,0:T(8,128)S(1)} %add_add_fusion.3), channel_id=1, source_target_pairs={{0,32},{1,33},{2,34},{3,35},{4,36},{5,37},{6,38},{7,39},{8,40},{9,... | collective-permute-start | bytes 393224 | tf_op jit(solution)/shard_map/ppermute | solution.py:26
  143.0 7.3 %collective-permute-start.25 = (f32[256,512]{1,0:T(8,128)S(1)}, f32[256,512]{1,0:T(8,128)S(1)}, u32[]{:S(2)}, u32[]{:S(2)}) collective-permute-start(f32[256,512]{1,0:T(8,128)S(1)} %pad_maximum_fusion.1.refs_22_.near_ref), channel_id=1, source_target_pairs={{0,1},{1,0},{2,3},{3,2},{4,5},{5,4},{6,7},{7,6},{8,9},{9,8},{10,11... | collective-permute-start | bytes 1572872 | tf_op jit(solution)/shard_map/ppermute | solution.py:26
  174.4 7.1 %collective-permute-start.29 = (f32[64,512]{1,0:T(8,128)S(1)}, f32[64,512]{1,0:T(8,128)S(1)}, u32[]{:S(2)}, u32[]{:S(2)}) collective-permute-start(f32[64,512]{1,0:T(8,128)S(1)} %get-tuple-element.57), channel_id=1, source_target_pairs={{0,12},{1,13},{2,14},{3,15},{4,8},{5,9},{6,10},{7,11},{8,4},{9,5},... | collective-permute-start | bytes 393224 | tf_op jit(solution)/shard_map/ppermute | solution.py:26
  176.1 7.9 %collective-permute-start.27 = (f32[64,512]{1,0:T(8,128)S(1)}, f32[64,512]{1,0:T(8,128)S(1)}, u32[]{:S(2)}, u32[]{:S(2)}) collective-permute-start(f32[64,512]{1,0:T(8,128)S(1)} %get-tuple-element.59), channel_id=1, source_target_pairs={{0,8},{1,9},{2,10},{3,11},{4,12},{5,13},{6,14},{7,15},{8,0},{9,1},... | collective-permute-start | bytes 393224 | tf_op jit(solution)/shard_map/ppermute | solution.py:26
  185.9 6.3 %collective-permute-start.30 = (f32[64,512]{1,0:T(8,128)S(1)}, f32[64,512]{1,0:T(8,128)S(1)}, u32[]{:S(2)}, u32[]{:S(2)}) collective-permute-start(f32[64,512]{1,0:T(8,128)S(1)} %fusion), channel_id=1, source_target_pairs={{0,2},{1,3},{2,0},{3,1},{4,6},{5,7},{6,4},{7,5},{8,10},{9,11},{10,... | collective-permute-start | bytes 393224 | tf_op jit(solution)/shard_map/ppermute | solution.py:26
  207.3 7.4 %collective-permute-start.39 = (f32[256,512]{1,0:T(8,128)S(1)}, f32[256,512]{1,0:T(8,128)S(1)}, u32[]{:S(2)}, u32[]{:S(2)}) collective-permute-start(f32[256,512]{1,0:T(8,128)S(1)} %pad_maximum_fusion.2.near_ref), channel_id=1, source_target_pairs={{0,1},{1,0},{2,3},{3,2},{4,5},{5,4},{6,7},{7,6},{8,9},{9,8},{10,11... | collective-permute-start | bytes 1572872 | tf_op jit(solution)/shard_map/ppermute | solution.py:26
  (28 other events, 184.3 us)
where the time goes:
time: 222 us; the launch traced here: 219 us
  Pallas kernels  81.8 us (37%)
  starting transfers between devices  75.3 us (34%)
  waiting for transfers between devices  48.5 us (22%)
  local copies, waits for them, and re-layouts  8.68 us (4%)
  other arithmetic  4.24 us (2%)
    ppermute x40, starting transfers between devices, swap(): return lax.ppermute(v, BOTH, partners(dx, dyh, dcore, dyl, dz))  70 us
    ppermute x40, waiting for transfers between devices, swap(): return lax.ppermute(v, BOTH, partners(dx, dyh, dcore, dyl, dz))  45.4 us
    pallas_call x2, Pallas kernels, step(): pl.pallas_call(kernel, out_shape=[half, half], grid=(5,), in_specs=[in_sm...  39.5 us
    pallas_call x4, Pallas kernels, sort_codes(): pl.pallas_call(sort_kernel, out_shape=[jax.ShapeDtypeStruct((2, 264, 128)...  21.1 us
    pallas_call x1, Pallas kernels, split_hessian(): pl.pallas_call(split_kernel, out_shape=jax.ShapeDtypeStruct((8, 512, 1024...  10.5 us
    pallas_call x2, Pallas kernels, update(): pl.pallas_call(update_kernel, out_shape=jax.ShapeDtypeStruct((512, 2, 256...  6.35 us
    all_to_all x1, starting transfers between devices, per_device(): pieces = lax.all_to_all(pieces, 'col', 0, 0, tiled=True)  5.27 us
    slice x16, local copies, waits for them, and re-layouts, per_device(): book_col = jnp.concatenate([v[:, :, 96:98, 0] for v in around])  5.08 us
  transfers between devices with their start and end apart: 41, of which 25 were waited for; matrix products, arithmetic and copies ran while one was open for 4% of the time, Pallas kernels for 16%

commit v1 on v0

--- a/solution.py
+++ b/solution.py
@@ -241,8 +241,8 @@
 def step_body(second, where_ref, packed_refs, rights, refs):
     error_refs, refs = (refs[:8], refs[8:16]), refs[16:]
     if second:
-        (near_ref, far_ref, book_col_ref), refs = refs[:3], refs[3:]
-    keep_ref, send_ref, left0_ref, left1_ref, grad_ref, sums_ref, table_ref = refs
+        (near_ref, far_ref), refs = refs[:2], refs[2:]
+    keep_ref, send_ref, left0_ref, left1_ref, grad_ref, sums_ref, high_ref, low_ref, ids_ref, table_ref = refs
     n = pl.program_id(0)
     row, col, place = where_ref[0], where_ref[1], where_ref[2]
 
@@ -256,18 +256,27 @@
                 grad_ref[2 * part + 1, rows, :] += more[:, 128:256]
 
     def prepare(half, left_ref):
-        b = jnp.minimum(2 * n + half, 7)
+        if second:
+            for which in range(8):
+                for kyh in range(2):
+                    at = which * 4 + kyh * 2
+                    ids_ref[half, at : at + 2, :] = error_refs[half][which][kyh, 0, 96:98, :]
+            ids = ids_ref[half].astype(I32) ^ place
+            lane = iota((32, 128), 1)
+            chosen = [jnp.where(ids == lane + k * 128, 1.0, 0.0) for k in range(4)]
+            chosen = jnp.concatenate(chosen, axis=1).astype(BF16)
+            table_ref[half] = LEARN_RATE * (dot_nn(chosen, high_ref[...]) + dot_nn(chosen, low_ref[...]))
         for core in range(2):
             for kx in range(4):
                 which = core * 4 + kx
                 for kyh in range(2):
                     start = pl.multiple_of((col ^ (kx * 4 + kyh * 2 + core)) * 16, 16)
-                    base = core * 16 + (kx * 2 + kyh) * 2
+                    base = which * 4 + kyh * 2
                     for c in range(2):
                         if second:
                             tables = [
                                 [
-                                    jnp.broadcast_to(table_ref[b, base + t : base + t + 1, (c * 2 + k) * 128 : (c * 2 + k) * 128 + 128], (8, 128))
+                                    jnp.broadcast_to(table_ref[half, base + t : base + t + 1, (c * 2 + k) * 128 : (c * 2 + k) * 128 + 128], (8, 128))
                                     for k in range(2)
                                 ]
                                 for t in range(2)
@@ -291,13 +300,8 @@
         left1_ref[...] = jnp.zeros((512, 768), BF16)
         grad_ref[...] = jnp.zeros((8, 512, 128), F32)
         if second:
-            chosen = jnp.where((book_col_ref[...] ^ place) == iota((256, 512), 1), 1.0, 0.0).astype(BF16)
-            total = jnp.zeros((256, 512), F32)
-            for part, ref in ((0, near_ref), (1, far_ref)):
-                high, low = split(ref[...])
-                here = chosen[:, part * 256 : part * 256 + 256]
-                total = total + dot_nn(here, high) + dot_nn(here, low)
-            table_ref[...] = (total * LEARN_RATE).reshape(8, 32, 512)
+            high_ref[0:256, :], low_ref[0:256, :] = split(near_ref[...])
+            high_ref[256:512, :], low_ref[256:512, :] = split(far_ref[...])
 
     prepare(0, left0_ref)
     multiply(left1_ref, rights[0])
@@ -313,7 +317,8 @@
         running = jnp.where(spot_back(iota((256, 128), 0) & 127) <= iota((256, 128), 1), 1.0, 0.0).astype(BF16)
         lane = iota((32, 128), 1)
         for kz in range(4):
-            for dyl in range(2):
+
+            def sum_codes(dyl, carry, kz=kz):
                 j = row ^ (dyl * 4 + kz)
                 at = kz * 2 + dyl
                 both = jnp.concatenate([grad_ref[j, 0:256, :], grad_ref[j, 256:512, :]], axis=1)
@@ -334,6 +339,9 @@
                     high_sums = 2.0 * (upto[1] - jnp.where(lane == 0, earlier[0], earlier[1]))
                     sums_ref[at, :, c * 256 : c * 256 + 128] = low_sums
                     sums_ref[at, :, c * 256 + 128 : c * 256 + 256] = high_sums
+                return carry
+
+            lax.fori_loop(0, 2, sum_codes, 0)
         books = [packed_refs[kz][0, 256:257, :] + packed_refs[kz][1, 256:257, :] for kz in range(4)]
         books = jnp.concatenate([books[0] + books[1], books[2] + books[3]], axis=1)
         chosen = jnp.where((iota((512, 256), 0) ^ place) == books, 1.0, 0.0).astype(BF16)
@@ -372,7 +380,10 @@
             pltpu.VMEM((512, 768), BF16),
             pltpu.VMEM((8, 512, 128), F32),
             pltpu.VMEM((8, 32, 512), F32),
-            pltpu.VMEM((8, 32, 512), F32),
+            pltpu.VMEM((512, 512), BF16),
+            pltpu.VMEM((512, 512), BF16),
+            pltpu.VMEM((2, 32, 128), F32),
+            pltpu.VMEM((2, 32, 512), F32),
         ],
         compiler_params=pltpu.CompilerParams(vmem_limit_bytes=VMEM_LIMIT),
         cost_estimate=pl.CostEstimate(flops=STEP_FLOPS, bytes_accessed=16 * 1024 * 1024, transcendentals=0),
@@ -397,18 +408,18 @@
     )(where, codebooks, near, far)
 
 
-def sum_all(keep, send, beside):
+def sum_all(keep, send, *beside):
     half = keep + swap(send, dcore=1)
     quarter = [half[k * 64 : k * 64 + 64] for k in range(4)]
     got = [None] + [swap(quarter[k], dx=k) for k in (1, 2, 3)]
     s = (quarter[0] + got[2]) + (got[1] + got[3])
-    s, beside = hold(s, beside)
+    s, *beside = hold(s, *beside)
     got = [None] + [swap(s, dyl=k & 1, dyh=k >> 1) for k in (1, 2, 3)]
     s = (s + got[2]) + (got[1] + got[3])
     got = [None] + [swap(s, dz=k) for k in (1, 2, 3)]
     s = (s + got[2]) + (got[1] + got[3])
     near = jnp.concatenate([s] + [swap(s, dx=k) for k in (1, 2, 3)])
-    return near, swap(near, dcore=1), beside
+    return near, swap(near, dcore=1), *beside
 
 
 def hold(*values):
@@ -448,10 +459,8 @@
     around = both_cores(around)
     packed = [*packed, *packed_one, *sort_codes([two], 2), *packed_three]
     keep, send = step(False, where, packed, right, around, [])
-    book_col = jnp.concatenate([v[:, :, 96:98, 0] for v in around])
-    book_col = book_col.transpose(1, 0, 2).reshape(256, 1).astype(I32)
-    near, far, book_col = sum_all(keep, send, book_col)
-    keep, send = step(True, where, packed, right, around, [near, far, book_col])
+    near, far = sum_all(keep, send)
+    keep, send = step(True, where, packed, right, around, [near, far])
     near, far, codebooks = sum_all(keep, send, update(where, codebooks, near, far))
     return update(where, codebooks, near, far)
 

time: 222 us -> 214 us (0.964); the launches traced: 219 us -> 213 us
  starting transfers between devices: 75.3 us -> 65.3 us
  Pallas kernels: 81.8 us -> 87.6 us
  local copies, waits for them, and re-layouts: 8.68 us -> 4.87 us
  waiting for transfers between devices: 48.5 us -> 50.8 us
    ppermute x40, starting transfers between devices: 70 us -> 60 us  [swap(): return lax.ppermute(v, BOTH, partners(dx, dyh, dcore, dyl, dz))]
    pallas_call x2, Pallas kernels: 39.5 us -> 45.3 us  [step(): pl.pallas_call(kernel, out_shape=[half, half], grid=(5,), in_specs=[in_sm...]
    slice x16 -> x0, local copies, waits for them, and re-layouts: 5.08 us -> none  [per_device(): book_col = jnp.concatenate([v[:, :, 96:98, 0] for v in around])]
    unnamed x29 -> x32, local copies, waits for them, and re-layouts: 2.42 us -> 4.81 us
    ppermute x40, waiting for transfers between devices: 45.4 us -> 47.8 us  [swap(): return lax.ppermute(v, BOTH, partners(dx, dyh, dcore, dyl, dz))]
  transfers between devices with their start and end apart: 41 -> 41, of which waited for: 25 -> 28; matrix products, arithmetic and copies ran while one was open for 4% -> 1% of each run, Pallas kernels for 16% -> 16%
where the time goes in v1:
time: 214 us; the launch traced here: 213 us
  Pallas kernels  87.6 us (41%)
  starting transfers between devices  65.3 us (31%)
  waiting for transfers between devices  50.8 us (24%)
  local copies, waits for them, and re-layouts  4.87 us (2%)
  other arithmetic  4.29 us (2%)
    ppermute x40, starting transfers between devices, swap(): return lax.ppermute(v, BOTH, partners(dx, dyh, dcore, dyl, dz))  60 us
    ppermute x40, waiting for transfers between devices, swap(): return lax.ppermute(v, BOTH, partners(dx, dyh, dcore, dyl, dz))  47.8 us
    pallas_call x2, Pallas kernels, step(): pl.pallas_call(kernel, out_shape=[half, half], grid=(5,), in_specs=[in_sm...  45.3 us
    pallas_call x4, Pallas kernels, sort_codes(): pl.pallas_call(sort_kernel, out_shape=[jax.ShapeDtypeStruct((2, 264, 128)...  21.1 us
    pallas_call x1, Pallas kernels, split_hessian(): pl.pallas_call(split_kernel, out_shape=jax.ShapeDtypeStruct((8, 512, 1024...  10.5 us
    pallas_call x2, Pallas kernels, update(): pl.pallas_call(update_kernel, out_shape=jax.ShapeDtypeStruct((512, 2, 256...  6.38 us
    all_to_all x1, starting transfers between devices, per_device(): pieces = lax.all_to_all(pieces, 'col', 0, 0, tiled=True)  5.26 us
    unnamed x32, local copies, waits for them, and re-layouts  4.81 us
  transfers between devices with their start and end apart: 41, of which 28 were waited for; matrix products, arithmetic and copies ran while one was open for 1% of the time, Pallas kernels for 16%

profile of v1, /device:TPU:1, one launch (start us, length us, event | category | flops | bytes accessed | tf_op | source)
XLA Modules:
  0.0 213.1 jit_solution(13058435328734892561)
XLA Ops:
  1.7 2.6 %shard_map.56 = f32[8,104,128]{2,1,0:T(8,128)} custom-call(s32[2,8]{1,0:T(2,128)} %tile_ref.3, bf16[32,2048]{1,0:T(8,128)(2,1)} %weights_ref.1, s32[32,1024]{1,0:T(8,128)} %get-tuple-element.30.own_ref, f32[512,2,256]{2,1,0:T(2,128)} %books_ref.3), custom_call_target="tpu_custom_call" | custom-call | tf_op jit(solution)/shard_map/pallas_call | solution.py:130
  4.3 3.7 %collective-permute-start = (f32[8,104,128]{2,1,0:T(8,128)}, f32[8,104,128]{2,1,0:T(8,128)S(1)}, u32[]{:S(2)}, u32[]{:S(2)}) collective-permute-start(f32[8,104,128]{2,1,0:T(8,128)} %shard_map.56), channel_id=1, source_target_pairs={{0,2},{1,3},{2,0},{3,1},{4,6},{5,7},{6,4},{7,5},{8,10},{9,11},{10,... | collective-permute-start | bytes 1277960 | tf_op jit(solution)/shard_map/ppermute | solution.py:26
  8.0 5.3 %all-to-all-start = ((s32[16,24,128]{2,1,0:T(8,128)}), s32[16,24,128]{2,1,0:T(8,128)S(1)}, u32[]{:S(2)}, u32[]{:S(2)}) async-start(s32[16,24,128]{2,1,0:T(8,128)} %get-tuple-element.29), calls=%async_computation | async-start | bytes 393216 | tf_op jit(solution)/shard_map/all_to_all | solution.py:445
  13.3 4.2 %collective-permute-done = f32[8,104,128]{2,1,0:T(8,128)S(1)} collective-permute-done((f32[8,104,128]{2,1,0:T(8,128)}, f32[8,104,128]{2,1,0:T(8,128)S(1)}, u32[]{:S(2)}, u32[]{:S(2)}) %collective-permute-start) | collective-permute-done | bytes 426016 | tf_op jit(solution)/shard_map/ppermute | solution.py:26
  18.6 3.0 %all-to-all-done = s32[16,24,128]{2,1,0:T(8,128)S(1)} async-done(((s32[16,24,128]{2,1,0:T(8,128)}), s32[16,24,128]{2,1,0:T(8,128)S(1)}, u32[]{:S(2)}, u32[]{:S(2)}) %all-to-all-start) | async-done | bytes 196640 | tf_op jit(solution)/shard_map/all_to_all | solution.py:445
  27.7 3.8 %collective-permute-start.3 = (s32[2,16,24,128]{3,2,1,0:T(8,128)S(1)}, s32[2,16,24,128]{3,2,1,0:T(8,128)S(1)}, u32[]{:S(2)}, u32[]{:S(2)}) collective-permute-start(s32[2,16,24,128]{3,2,1,0:T(8,128)S(1)} %pad_add_fusion.refs_0_), channel_id=1, source_target_pairs={{0,48},{1,49},{2,50},{3,51},{4,52},{5,53},{6,54},{7,55},{8,56},{9,... | collective-permute-start | bytes 1179656 | tf_op jit(solution)/shard_map/ppermute | solution.py:26
  31.5 10.5 %shard_map.57.refs_4_.refs_5_ = bf16[8,512,1024]{2,1,0:T(8,128)(2,1)} custom-call(s32[3]{0:T(128)} %pad_add_fusion.1.where_ref, f32[16384,128]{1,0:T(8,128)} %bitcast.12), custom_call_target="tpu_custom_call" | custom-call | flops 8999999488 | bytes 20971520 | tf_op jit(solution)/shard_map/pallas_call | solution.py:230
  42.1 5.3 %shard_map.58.refs_0_ = s32[2,264,128]{2,1,0:T(8,128)} custom-call(s32[2,16,24,128]{3,2,1,0:T(8,128)} %copy-done.5), custom_call_target="tpu_custom_call" | custom-call | flops 5000000000 | bytes 1048576 | tf_op jit(solution)/shard_map/pallas_call | solution.py:209
  48.7 5.3 %shard_map.59.refs_1_ = s32[2,264,128]{2,1,0:T(8,128)} custom-call(s32[2,16,24,128]{3,2,1,0:T(8,128)} %copy-done.15), custom_call_target="tpu_custom_call" | custom-call | flops 5000000000 | bytes 1048576 | tf_op jit(solution)/shard_map/pallas_call | solution.py:209
  54.0 5.3 %shard_map.60.refs_3_ = s32[2,264,128]{2,1,0:T(8,128)} custom-call(s32[2,16,24,128]{3,2,1,0:T(8,128)} %copy-done.14), custom_call_target="tpu_custom_call" | custom-call | flops 5000000000 | bytes 1048576 | tf_op jit(solution)/shard_map/pallas_call | solution.py:209
  59.3 3.3 %collective-permute-done.6.refs_9_.refs_17_ = f32[2,8,104,128]{3,2,1,0:T(8,128)S(1)} collective-permute-done((f32[2,8,104,128]{3,2,1,0:T(8,128)S(1)}, f32[2,8,104,128]{3,2,1,0:T(8,128)S(1)}, u32[]{:S(2)}, u32[]{:S(2)}) %collective-permute-start.6) | collective-permute-done | bytes 852000 | tf_op jit(solution)/shard_map/ppermute | solution.py:26
  66.1 5.3 %shard_map.61.refs_2_ = s32[2,264,128]{2,1,0:T(8,128)} custom-call(s32[2,16,24,128]{3,2,1,0:T(8,128)} %copy-done.13), custom_call_target="tpu_custom_call" | custom-call | flops 5000000000 | bytes 1048576 | tf_op jit(solution)/shard_map/pallas_call | solution.py:209
  73.9 21.9 %shard_map.62 = (f32[256,512]{1,0:T(8,128)}, f32[256,512]{1,0:T(8,128)}) custom-call(s32[3]{0:T(128)} %pad_add_fusion.1.where_ref, s32[2,264,128]{2,1,0:T(8,128)} %shard_map.58.refs_0_, s32[2,264,128]{2,1,0:T(8,128)} %shard_map.59.refs_1_, s32[2,264,128]{2,1,0:T(8,128)} %shard_map.61.refs_2_, s32[2,264,128]{2,1,0:T(8,128)} %shard_map.60.refs_3_, ...), custom_call_target="tpu_custom_call" | custom-call | flops 17999998976 | bytes 16777216 | tf_op jit(solution)/shard_map/pallas_call | solution.py:368
  105.4 3.4 %collective-permute-done.13 = f32[64,512]{1,0:T(8,128)S(1)} collective-permute-done((f32[64,512]{1,0:T(8,128)S(1)}, f32[64,512]{1,0:T(8,128)S(1)}, u32[]{:S(2)}, u32[]{:S(2)}) %collective-permute-start.13) | collective-permute-done | bytes 131104 | tf_op jit(solution)/shard_map/ppermute | solution.py:26
  110.4 2.4 %collective-permute-start.16 = (f32[64,512]{1,0:T(8,128)S(1)}, f32[64,512]{1,0:T(8,128)S(1)}, u32[]{:S(2)}, u32[]{:S(2)}) collective-permute-start(f32[64,512]{1,0:T(8,128)S(1)} %fusion.1), channel_id=1, source_target_pairs={{0,2},{1,3},{2,0},{3,1},{4,6},{5,7},{6,4},{7,5},{8,10},{9,11},{10,... | collective-permute-start | bytes 393224 | tf_op jit(solution)/shard_map/ppermute | solution.py:26
  114.0 3.1 %collective-permute-done.16 = f32[64,512]{1,0:T(8,128)S(1)} collective-permute-done((f32[64,512]{1,0:T(8,128)S(1)}, f32[64,512]{1,0:T(8,128)S(1)}, u32[]{:S(2)}, u32[]{:S(2)}) %collective-permute-start.16) | collective-permute-done | bytes 131104 | tf_op jit(solution)/shard_map/ppermute | solution.py:26
  117.1 3.8 %collective-permute-start.21 = (f32[64,512]{1,0:T(8,128)S(1)}, f32[64,512]{1,0:T(8,128)S(1)}, u32[]{:S(2)}, u32[]{:S(2)}) collective-permute-start(f32[64,512]{1,0:T(8,128)S(1)} %add_add_fusion.3), channel_id=1, source_target_pairs={{0,48},{1,49},{2,50},{3,51},{4,52},{5,53},{6,54},{7,55},{8,56},{9,... | collective-permute-start | bytes 393224 | tf_op jit(solution)/shard_map/ppermute | solution.py:26
  133.6 6.1 %collective-permute-start.25 = (f32[256,512]{1,0:T(8,128)S(1)}, f32[256,512]{1,0:T(8,128)S(1)}, u32[]{:S(2)}, u32[]{:S(2)}) collective-permute-start(f32[256,512]{1,0:T(8,128)S(1)} %pad_maximum_fusion.1.refs_22_.near_ref), channel_id=1, source_target_pairs={{0,1},{1,0},{2,3},{3,2},{4,5},{5,4},{6,7},{7,6},{8,9},{9,8},{10,11... | collective-permute-start | bytes 1572872 | tf_op jit(solution)/shard_map/ppermute | solution.py:26
  142.1 23.4 %shard_map.63 = (f32[256,512]{1,0:T(8,128)}, f32[256,512]{1,0:T(8,128)}) custom-call(s32[3]{0:T(128)} %pad_add_fusion.1.where_ref, s32[2,264,128]{2,1,0:T(8,128)} %shard_map.58.refs_0_, s32[2,264,128]{2,1,0:T(8,128)} %shard_map.59.refs_1_, s32[2,264,128]{2,1,0:T(8,128)} %shard_map.61.refs_2_, s32[2,264,128]{2,1,0:T(8,128)} %shard_map.60.refs_3_, ...), custom_call_target="tpu_custom_call" | custom-call | flops 17999998976 | bytes 16777216 | tf_op jit(solution)/shard_map/pallas_call | solution.py:368
  172.8 3.2 %shard_map.64.books_ref = f32[512,2,256]{2,1,0:T(2,128)} custom-call(s32[3]{0:T(128)} %pad_add_fusion.1.where_ref, f32[512,2,256]{2,1,0:T(2,128)} %books_ref.3, f32[256,512]{1,0:T(8,128)} %copy-done, f32[256,512]{1,0:T(8,128)} %copy-done.3), custom_call_target="tpu_custom_call" | custom-call | tf_op jit(solution)/shard_map/pallas_call | solution.py:403
  176.0 2.5 %collective-permute-done.27 = f32[64,512]{1,0:T(8,128)S(1)} collective-permute-done((f32[64,512]{1,0:T(8,128)S(1)}, f32[64,512]{1,0:T(8,128)S(1)}, u32[]{:S(2)}, u32[]{:S(2)}) %collective-permute-start.27) | collective-permute-done | bytes 131104 | tf_op jit(solution)/shard_map/ppermute | solution.py:26
  184.2 2.5 %collective-permute-done.30 = f32[64,512]{1,0:T(8,128)S(1)} collective-permute-done((f32[64,512]{1,0:T(8,128)S(1)}, f32[64,512]{1,0:T(8,128)S(1)}, u32[]{:S(2)}, u32[]{:S(2)}) %collective-permute-start.30) | collective-permute-done | bytes 131104 | tf_op jit(solution)/shard_map/ppermute | solution.py:26
  201.7 5.9 %collective-permute-start.39 = (f32[256,512]{1,0:T(8,128)S(1)}, f32[256,512]{1,0:T(8,128)S(1)}, u32[]{:S(2)}, u32[]{:S(2)}) collective-permute-start(f32[256,512]{1,0:T(8,128)S(1)} %pad_maximum_fusion.2.near_ref), channel_id=1, source_target_pairs={{0,1},{1,0},{2,3},{3,2},{4,5},{5,4},{6,7},{7,6},{8,9},{9,8},{10,11... | collective-permute-start | bytes 1572872 | tf_op jit(solution)/shard_map/ppermute | solution.py:26
  209.9 3.2 %shard_map.65 = f32[512,2,256]{2,1,0:T(2,128)} custom-call(s32[3]{0:T(128)} %pad_add_fusion.1.where_ref, f32[512,2,256]{2,1,0:T(2,128)} %shard_map.64.books_ref, f32[256,512]{1,0:T(8,128)} %copy-done.1, f32[256,512]{1,0:T(8,128)} %copy-done.4), custom_call_target="tpu_custom_call" | custom-call | tf_op jit(solution)/shard_map/pallas_call | solution.py:403
  (116 shorter events, 74.0 us)
Async XLA Ops:
  4.3 13.2 %collective-permute-start = (f32[8,104,128]{2,1,0:T(8,128)}, f32[8,104,128]{2,1,0:T(8,128)S(1)}, u32[]{:S(2)}, u32[]{:S(2)}) collective-permute-start(f32[8,104,128]{2,1,0:T(8,128)} %shard_map.56), channel_id=1, source_target_pairs={{0,2},{1,3},{2,0},{3,1},{4,6},{5,7},{6,4},{7,5},{8,10},{9,11},{10,... | collective-permute-start | bytes 1277960 | tf_op jit(solution)/shard_map/ppermute | solution.py:26
  8.0 13.6 %all-to-all-start = ((s32[16,24,128]{2,1,0:T(8,128)}), s32[16,24,128]{2,1,0:T(8,128)S(1)}, u32[]{:S(2)}, u32[]{:S(2)}) async-start(s32[16,24,128]{2,1,0:T(8,128)} %get-tuple-element.29), calls=%async_computation | async-start | bytes 393216 | tf_op jit(solution)/shard_map/all_to_all | solution.py:445
  21.6 6.1 %collective-permute-start.1 = (s32[16,24,128]{2,1,0:T(8,128)S(1)}, s32[16,24,128]{2,1,0:T(8,128)S(1)}, u32[]{:S(2)}, u32[]{:S(2)}) collective-permute-start(s32[16,24,128]{2,1,0:T(8,128)S(1)} %all-to-all-done), channel_id=1, source_target_pairs={{0,64},{1,65},{2,66},{3,67},{4,68},{5,69},{6,70},{7,71},{8,72},{9,... | collective-permute-start | bytes 589832 | tf_op jit(solution)/shard_map/ppermute | solution.py:26
  23.3 39.3 %collective-permute-start.6 = (f32[2,8,104,128]{3,2,1,0:T(8,128)S(1)}, f32[2,8,104,128]{3,2,1,0:T(8,128)S(1)}, u32[]{:S(2)}, u32[]{:S(2)}) collective-permute-start(f32[2,8,104,128]{3,2,1,0:T(8,128)S(1)} %pad_maximum_fusion.refs_6_.refs_14_), channel_id=1, source_target_pairs={{0,12},{1,13},{2,14},{3,15},{4,8},{5,9},{6,10},{7,11},{8,4},{9,5},... | collective-permute-start | bytes 2555912 | tf_op jit(solution)/shard_map/ppermute | solution.py:26
  25.1 37.5 %collective-permute-start.5 = (f32[2,8,104,128]{3,2,1,0:T(8,128)S(1)}, f32[2,8,104,128]{3,2,1,0:T(8,128)S(1)}, u32[]{:S(2)}, u32[]{:S(2)}) collective-permute-start(f32[2,8,104,128]{3,2,1,0:T(8,128)S(1)} %pad_maximum_fusion.refs_6_.refs_14_), channel_id=1, source_target_pairs={{0,8},{1,9},{2,10},{3,11},{4,12},{5,13},{6,14},{7,15},{8,0},{9,1},... | collective-permute-start | bytes 2555912 | tf_op jit(solution)/shard_map/ppermute | solution.py:26
  25.6 37.3 %collective-permute-start.4 = (f32[2,8,104,128]{3,2,1,0:T(8,128)S(1)}, f32[2,8,104,128]{3,2,1,0:T(8,128)S(1)}, u32[]{:S(2)}, u32[]{:S(2)}) collective-permute-start(f32[2,8,104,128]{3,2,1,0:T(8,128)S(1)} %pad_maximum_fusion.refs_6_.refs_14_), channel_id=1, source_target_pairs={{0,4},{1,5},{2,6},{3,7},{4,0},{5,1},{6,2},{7,3},{8,12},{9,13},{10,... | collective-permute-start | bytes 2555912 | tf_op jit(solution)/shard_map/ppermute | solution.py:26
  27.7 19.6 %collective-permute-start.3 = (s32[2,16,24,128]{3,2,1,0:T(8,128)S(1)}, s32[2,16,24,128]{3,2,1,0:T(8,128)S(1)}, u32[]{:S(2)}, u32[]{:S(2)}) collective-permute-start(s32[2,16,24,128]{3,2,1,0:T(8,128)S(1)} %pad_add_fusion.refs_0_), channel_id=1, source_target_pairs={{0,48},{1,49},{2,50},{3,51},{4,52},{5,53},{6,54},{7,55},{8,56},{9,... | collective-permute-start | bytes 1179656 | tf_op jit(solution)/shard_map/ppermute | solution.py:26
  31.5 15.8 %collective-permute-start.2 = (s32[2,16,24,128]{3,2,1,0:T(8,128)S(1)}, s32[2,16,24,128]{3,2,1,0:T(8,128)S(1)}, u32[]{:S(2)}, u32[]{:S(2)}) collective-permute-start(s32[2,16,24,128]{3,2,1,0:T(8,128)S(1)} %pad_add_fusion.refs_0_), channel_id=1, source_target_pairs={{0,16},{1,17},{2,18},{3,19},{4,20},{5,21},{6,22},{7,23},{8,24},{9,... | collective-permute-start | bytes 1179656 | tf_op jit(solution)/shard_map/ppermute | solution.py:26
  47.3 18.0 %collective-permute-start.7 = (s32[2,16,24,128]{3,2,1,0:T(8,128)}, s32[2,16,24,128]{3,2,1,0:T(8,128)S(1)}, u32[]{:S(2)}, u32[]{:S(2)}) collective-permute-start(s32[2,16,24,128]{3,2,1,0:T(8,128)} %copy-done.5), channel_id=1, source_target_pairs={{0,32},{1,33},{2,34},{3,35},{4,36},{5,37},{6,38},{7,39},{8,40},{9,... | collective-permute-start | bytes 1179656 | tf_op jit(solution)/shard_map/ppermute | solution.py:26
  62.9 8.5 %collective-permute-start.8 = (f32[2,8,104,128]{3,2,1,0:T(8,128)S(1)}, f32[2,8,104,128]{3,2,1,0:T(8,128)S(1)}, u32[]{:S(2)}, u32[]{:S(2)}) collective-permute-start(f32[2,8,104,128]{3,2,1,0:T(8,128)S(1)} %pad_maximum_fusion.refs_6_.refs_14_), channel_id=1, source_target_pairs={{0,1},{1,0},{2,3},{3,2},{4,5},{5,4},{6,7},{7,6},{8,9},{9,8},{10,11... | collective-permute-start | bytes 2555912 | tf_op jit(solution)/shard_map/ppermute | solution.py:26
  64.8 6.7 %collective-permute-start.9 = (f32[2,8,104,128]{3,2,1,0:T(8,128)S(1)}, f32[2,8,104,128]{3,2,1,0:T(8,128)S(1)}, u32[]{:S(2)}, u32[]{:S(2)}) collective-permute-start(f32[2,8,104,128]{3,2,1,0:T(8,128)S(1)} %collective-permute-done.4.refs_7_.refs_15_), channel_id=1, source_target_pairs={{0,1},{1,0},{2,3},{3,2},{4,5},{5,4},{6,7},{7,6},{8,9},{9,8},{10,11... | collective-permute-start | bytes 2555912 | tf_op jit(solution)/shard_map/ppermute | solution.py:26
  64.9 6.6 %collective-permute-start.10 = (f32[2,8,104,128]{3,2,1,0:T(8,128)S(1)}, f32[2,8,104,128]{3,2,1,0:T(8,128)S(1)}, u32[]{:S(2)}, u32[]{:S(2)}) collective-permute-start(f32[2,8,104,128]{3,2,1,0:T(8,128)S(1)} %collective-permute-done.5.refs_8_.refs_16_), channel_id=1, source_target_pairs={{0,1},{1,0},{2,3},{3,2},{4,5},{5,4},{6,7},{7,6},{8,9},{9,8},{10,11... | collective-permute-start | bytes 2555912 | tf_op jit(solution)/shard_map/ppermute | solution.py:26
  65.3 6.2 %collective-permute-start.11 = (f32[2,8,104,128]{3,2,1,0:T(8,128)S(1)}, f32[2,8,104,128]{3,2,1,0:T(8,128)S(1)}, u32[]{:S(2)}, u32[]{:S(2)}) collective-permute-start(f32[2,8,104,128]{3,2,1,0:T(8,128)S(1)} %collective-permute-done.6.refs_9_.refs_17_), channel_id=1, source_target_pairs={{0,1},{1,0},{2,3},{3,2},{4,5},{5,4},{6,7},{7,6},{8,9},{9,8},{10,11... | collective-permute-start | bytes 2555912 | tf_op jit(solution)/shard_map/ppermute | solution.py:26
  99.2 6.0 %collective-permute-start.15 = (f32[64,512]{1,0:T(8,128)S(1)}, f32[64,512]{1,0:T(8,128)S(1)}, u32[]{:S(2)}, u32[]{:S(2)}) collective-permute-start(f32[64,512]{1,0:T(8,128)S(1)} %get-tuple-element.56), channel_id=1, source_target_pairs={{0,12},{1,13},{2,14},{3,15},{4,8},{5,9},{6,10},{7,11},{8,4},{9,5},... | collective-permute-start | bytes 393224 | tf_op jit(solution)/shard_map/ppermute | solution.py:26
  101.0 7.8 %collective-permute-start.13 = (f32[64,512]{1,0:T(8,128)S(1)}, f32[64,512]{1,0:T(8,128)S(1)}, u32[]{:S(2)}, u32[]{:S(2)}) collective-permute-start(f32[64,512]{1,0:T(8,128)S(1)} %get-tuple-element.58), channel_id=1, source_target_pairs={{0,8},{1,9},{2,10},{3,11},{4,12},{5,13},{6,14},{7,15},{8,0},{9,1},... | collective-permute-start | bytes 393224 | tf_op jit(solution)/shard_map/ppermute | solution.py:26
  110.4 6.6 %collective-permute-start.16 = (f32[64,512]{1,0:T(8,128)S(1)}, f32[64,512]{1,0:T(8,128)S(1)}, u32[]{:S(2)}, u32[]{:S(2)}) collective-permute-start(f32[64,512]{1,0:T(8,128)S(1)} %fusion.1), channel_id=1, source_target_pairs={{0,2},{1,3},{2,0},{3,1},{4,6},{5,7},{6,4},{7,5},{8,10},{9,11},{10,... | collective-permute-start | bytes 393224 | tf_op jit(solution)/shard_map/ppermute | solution.py:26
  117.1 6.2 %collective-permute-start.21 = (f32[64,512]{1,0:T(8,128)S(1)}, f32[64,512]{1,0:T(8,128)S(1)}, u32[]{:S(2)}, u32[]{:S(2)}) collective-permute-start(f32[64,512]{1,0:T(8,128)S(1)} %add_add_fusion.3), channel_id=1, source_target_pairs={{0,48},{1,49},{2,50},{3,51},{4,52},{5,53},{6,54},{7,55},{8,56},{9,... | collective-permute-start | bytes 393224 | tf_op jit(solution)/shard_map/ppermute | solution.py:26
  120.9 5.4 %collective-permute-start.19 = (f32[64,512]{1,0:T(8,128)S(1)}, f32[64,512]{1,0:T(8,128)S(1)}, u32[]{:S(2)}, u32[]{:S(2)}) collective-permute-start(f32[64,512]{1,0:T(8,128)S(1)} %add_add_fusion.3), channel_id=1, source_target_pairs={{0,32},{1,33},{2,34},{3,35},{4,36},{5,37},{6,38},{7,39},{8,40},{9,... | collective-permute-start | bytes 393224 | tf_op jit(solution)/shard_map/ppermute | solution.py:26
  133.6 7.6 %collective-permute-start.25 = (f32[256,512]{1,0:T(8,128)S(1)}, f32[256,512]{1,0:T(8,128)S(1)}, u32[]{:S(2)}, u32[]{:S(2)}) collective-permute-start(f32[256,512]{1,0:T(8,128)S(1)} %pad_maximum_fusion.1.refs_22_.near_ref), channel_id=1, source_target_pairs={{0,1},{1,0},{2,3},{3,2},{4,5},{5,4},{6,7},{7,6},{8,9},{9,8},{10,11... | collective-permute-start | bytes 1572872 | tf_op jit(solution)/shard_map/ppermute | solution.py:26
  168.8 7.2 %collective-permute-start.29 = (f32[64,512]{1,0:T(8,128)S(1)}, f32[64,512]{1,0:T(8,128)S(1)}, u32[]{:S(2)}, u32[]{:S(2)}) collective-permute-start(f32[64,512]{1,0:T(8,128)S(1)} %get-tuple-element.53), channel_id=1, source_target_pairs={{0,12},{1,13},{2,14},{3,15},{4,8},{5,9},{6,10},{7,11},{8,4},{9,5},... | collective-permute-start | bytes 393224 | tf_op jit(solution)/shard_map/ppermute | solution.py:26
  170.6 5.4 %collective-permute-start.28 = (f32[64,512]{1,0:T(8,128)S(1)}, f32[64,512]{1,0:T(8,128)S(1)}, u32[]{:S(2)}, u32[]{:S(2)}) collective-permute-start(f32[64,512]{1,0:T(8,128)S(1)} %get-tuple-element.54), channel_id=1, source_target_pairs={{0,4},{1,5},{2,6},{3,7},{4,0},{5,1},{6,2},{7,3},{8,12},{9,13},{10,... | collective-permute-start | bytes 393224 | tf_op jit(solution)/shard_map/ppermute | solution.py:26
  170.6 7.9 %collective-permute-start.27 = (f32[64,512]{1,0:T(8,128)S(1)}, f32[64,512]{1,0:T(8,128)S(1)}, u32[]{:S(2)}, u32[]{:S(2)}) collective-permute-start(f32[64,512]{1,0:T(8,128)S(1)} %get-tuple-element.55), channel_id=1, source_target_pairs={{0,8},{1,9},{2,10},{3,11},{4,12},{5,13},{6,14},{7,15},{8,0},{9,1},... | collective-permute-start | bytes 393224 | tf_op jit(solution)/shard_map/ppermute | solution.py:26
  180.4 6.3 %collective-permute-start.30 = (f32[64,512]{1,0:T(8,128)S(1)}, f32[64,512]{1,0:T(8,128)S(1)}, u32[]{:S(2)}, u32[]{:S(2)}) collective-permute-start(f32[64,512]{1,0:T(8,128)S(1)} %fusion), channel_id=1, source_target_pairs={{0,2},{1,3},{2,0},{3,1},{4,6},{5,7},{6,4},{7,5},{8,10},{9,11},{10,... | collective-permute-start | bytes 393224 | tf_op jit(solution)/shard_map/ppermute | solution.py:26
  201.7 7.4 %collective-permute-start.39 = (f32[256,512]{1,0:T(8,128)S(1)}, f32[256,512]{1,0:T(8,128)S(1)}, u32[]{:S(2)}, u32[]{:S(2)}) collective-permute-start(f32[256,512]{1,0:T(8,128)S(1)} %pad_maximum_fusion.2.near_ref), channel_id=1, source_target_pairs={{0,1},{1,0},{2,3},{3,2},{4,5},{5,4},{6,7},{7,6},{8,9},{9,8},{10,11... | collective-permute-start | bytes 1572872 | tf_op jit(solution)/shard_map/ppermute | solution.py:26
  (33 other events, 191.4 us)

commit v2 on v1

--- a/solution.py
+++ b/solution.py
@@ -177,16 +177,22 @@
     return jnp.concatenate(rows, axis=0)
 
 
-def sort_body(first_kz, *refs):
-    lane = iota((256, 128), 1)
-    spot32 = iota((8, 128), 1) >> 1
-    for n, (piece_ref, packed_ref) in enumerate(zip(refs[: len(refs) // 2], refs[len(refs) // 2 :])):
-        base = ((first_kz + n) % 2) * 32 + pl.program_id(0) * 16
+def sort_codes(pieces, odd_shift):
+    many = len(pieces)
+
+    def sort_kernel(*refs):
+        packed_ref = refs[many]
+        turn = pl.program_id(0)
+        piece = refs[0][0]
+        for n in range(1, many):
+            piece = jnp.where(turn >= 2 * n, refs[n][0], piece)
+        lane = iota((256, 128), 1)
+        base = odd_shift * 32 + lax.rem(turn, 2) * 16
         books = jnp.zeros((8, 128), I32)
         for origin in range(16):
-            books = jnp.where(spot32 == base + origin, piece_ref[0, origin, 16:24, :], books)
+            books = jnp.where((iota((8, 128), 1) >> 1) == base + origin, piece[origin, 16:24, :], books)
         packed_ref[0, 256:264, :] = books
-        key = (piece_ref[0, :, 0:16, :].reshape(256, 128) * 128 + lane).astype(F32)
+        key = (piece[:, 0:16, :].reshape(256, 128) * 128 + lane).astype(F32)
         halves = [sort_block(key[h * 128 : h * 128 + 128, :].T).T for h in range(2)]
         code = jnp.concatenate(halves, axis=0).astype(I32)
         counts = []
@@ -199,19 +205,12 @@
             counts.append(count)
         packed_ref[0, 0:256, :] = (code & 127) | (counts[0] << 8) | (counts[1] << 16)
 
-
-def sort_codes(pieces, first_kz):
-    many = len(pieces)
-
-    def sort_kernel(*refs):
-        sort_body(first_kz, *refs)
-
     return pl.pallas_call(
         sort_kernel,
-        out_shape=[jax.ShapeDtypeStruct((2, 264, 128), I32)] * many,
-        grid=(2,),
-        in_specs=[pl.BlockSpec((1, 16, 24, 128), lambda j: (j, 0, 0, 0))] * many,
-        out_specs=[pl.BlockSpec((1, 264, 128), lambda j: (j, 0, 0))] * many,
+        out_shape=jax.ShapeDtypeStruct((2 * many, 264, 128), I32),
+        grid=(2 * many,),
+        in_specs=[pl.BlockSpec((1, 16, 24, 128), lambda j, n=n: (jnp.clip(j - 2 * n, 0, 1), 0, 0, 0)) for n in range(many)],
+        out_specs=pl.BlockSpec((1, 264, 128), lambda j: (j, 0, 0)),
         compiler_params=pltpu.CompilerParams(vmem_limit_bytes=VMEM_LIMIT),
         cost_estimate=pl.CostEstimate(flops=many * SORT_FLOPS, bytes_accessed=many * 1024 * 1024, transcendentals=0),
     )(*pieces)
@@ -317,14 +316,14 @@
         running = jnp.where(spot_back(iota((256, 128), 0) & 127) <= iota((256, 128), 1), 1.0, 0.0).astype(BF16)
         lane = iota((32, 128), 1)
         for kz in range(4):
-
-            def sum_codes(dyl, carry, kz=kz):
+            for dyl in range(2):
                 j = row ^ (dyl * 4 + kz)
                 at = kz * 2 + dyl
                 both = jnp.concatenate([grad_ref[j, 0:256, :], grad_ref[j, 256:512, :]], axis=1)
                 high, low = split(both)
                 pairs = dot_nn(high, parting) + dot_nn(low, parting)
-                packed = packed_refs[kz][dyl, 0:256, :]
+                held_ref, first_row = packed_refs[kz]
+                packed = held_ref[first_row + dyl, 0:256, :]
                 source = packed & 127
                 counts = [(packed >> 8) & 255, packed >> 16]
                 for c in range(2):
@@ -339,10 +338,7 @@
                     high_sums = 2.0 * (upto[1] - jnp.where(lane == 0, earlier[0], earlier[1]))
                     sums_ref[at, :, c * 256 : c * 256 + 128] = low_sums
                     sums_ref[at, :, c * 256 + 128 : c * 256 + 256] = high_sums
-                return carry
-
-            lax.fori_loop(0, 2, sum_codes, 0)
-        books = [packed_refs[kz][0, 256:257, :] + packed_refs[kz][1, 256:257, :] for kz in range(4)]
+        books = [ref[first_row, 256:257, :] + ref[first_row + 1, 256:257, :] for ref, first_row in packed_refs]
         books = jnp.concatenate([books[0] + books[1], books[2] + books[3]], axis=1)
         chosen = jnp.where((iota((512, 256), 0) ^ place) == books, 1.0, 0.0).astype(BF16)
         high, low = split(sums_ref[...].reshape(256, 512))
@@ -353,7 +349,8 @@
 
 def step(second, place, packed, right, errors, rest):
     def kernel(where_ref, *refs):
-        step_body(second, where_ref, refs[0:4], refs[4:6], refs[6:])
+        zero, odd, two = refs[0:3]
+        step_body(second, where_ref, ((zero, 0), (odd, 0), (two, 0), (odd, 2)), refs[3:5], refs[5:])
 
     def tile_column(half):
         return lambda n: jnp.clip(2 * n + half, 0, 7)
@@ -392,11 +389,16 @@
 
 def update_kernel(where_ref, books_ref, near_ref, far_ref, out_ref):
     for part, ref in enumerate((near_ref, far_ref)):
-        for k in range(4):
+
+        def block(k, carry, part=part, ref=ref):
             start = pl.multiple_of((part * 256 + k * 64) ^ where_ref[2], 64)
+            from_row = pl.multiple_of(k * 64, 64)
             for c in range(2):
-                moved = LEARN_RATE * ref[k * 64 : k * 64 + 64, c * 256 : c * 256 + 256]
+                moved = LEARN_RATE * ref[pl.ds(from_row, 64), c * 256 : c * 256 + 256]
                 out_ref[pl.ds(start, 64), c, :] = books_ref[pl.ds(start, 64), c, :] - moved
+            return carry
+
+        lax.fori_loop(0, 4, block, 0)
 
 
 def update(where, codebooks, near, far):
@@ -454,10 +456,9 @@
     right, packed, one, three = hold(right, packed, *[swap(pieces, dz=k) for k in (1, 3)])
     pieces, one = hold(pieces, one)
     two = swap(pieces, dz=2)
-    packed_one, packed_three = sort_codes([one], 1), sort_codes([three], 3)
-    packed_one, packed_three, *around = hold(packed_one, packed_three, *around)
+    packed_odd, *around = hold(sort_codes([one, three], 1), *around)
     around = both_cores(around)
-    packed = [*packed, *packed_one, *sort_codes([two], 2), *packed_three]
+    packed = [packed, packed_odd, sort_codes([two], 0)]
     keep, send = step(False, where, packed, right, around, [])
     near, far = sum_all(keep, send)
     keep, send = step(True, where, packed, right, around, [near, far])

time: 214 us -> 209 us (0.977)
  Pallas kernels: 87.6 us -> 81.9 us
    pallas_call x2, Pallas kernels: 45.3 us -> 40.9 us  [step(): pl.pallas_call(kernel, out_shape=[half, half], grid=(5,), in_specs=[in_sm...]
    pallas_call x4 -> x3, Pallas kernels: 21.1 us -> 19.7 us  [sort_codes(): pl.pallas_call(sort_kernel, out_shape=jax.ShapeDtypeStruct((2 * many, 264...]
  transfers between devices with their start and end apart: 41 -> 41, of which waited for: 28 -> 29; matrix products, arithmetic and copies ran while one was open for 1% -> 1% of each run, Pallas kernels for 16% -> 16%
where the time goes in v2:
time: 209 us
  Pallas kernels  81.9 us (39%)
  starting transfers between devices  65.3 us (31%)
  waiting for transfers between devices  52.2 us (25%)
  local copies, waits for them, and re-layouts  4.85 us (2%)
  other arithmetic  4.22 us (2%)
    ppermute x40, starting transfers between devices, swap(): return lax.ppermute(v, BOTH, partners(dx, dyh, dcore, dyl, dz))  60 us
    ppermute x40, waiting for transfers between devices, swap(): return lax.ppermute(v, BOTH, partners(dx, dyh, dcore, dyl, dz))  49.1 us
    pallas_call x2, Pallas kernels, step(): pl.pallas_call(kernel, out_shape=[half, half], grid=(5,), in_specs=[in_sm...  40.9 us
    pallas_call x3, Pallas kernels, sort_codes(): pl.pallas_call(sort_kernel, out_shape=jax.ShapeDtypeStruct((2 * many, 264...  19.7 us
    pallas_call x1, Pallas kernels, split_hessian(): pl.pallas_call(split_kernel, out_shape=jax.ShapeDtypeStruct((8, 512, 1024...  10.5 us
    pallas_call x2, Pallas kernels, update(): pl.pallas_call(update_kernel, out_shape=jax.ShapeDtypeStruct((512, 2, 256...  6.55 us
    all_to_all x1, starting transfers between devices, per_device(): pieces = lax.all_to_all(pieces, 'col', 0, 0, tiled=True)  5.27 us
    unnamed x32, local copies, waits for them, and re-layouts  4.79 us
  transfers between devices with their start and end apart: 41, of which 29 were waited for; matrix products, arithmetic and copies ran while one was open for 1% of the time, Pallas kernels for 16%

profile of v2, /device:TPU:1, one launch (start us, length us, event | category | flops | bytes accessed | tf_op | source)
XLA Modules:
  0.0 208.7 jit_solution(13125576372038613604)
XLA Ops:
  1.7 2.6 %shard_map.56 = f32[8,104,128]{2,1,0:T(8,128)} custom-call(s32[2,8]{1,0:T(2,128)} %tile_ref.3, bf16[32,2048]{1,0:T(8,128)(2,1)} %weights_ref.1, s32[32,1024]{1,0:T(8,128)} %get-tuple-element.29.own_ref, f32[512,2,256]{2,1,0:T(2,128)} %books_ref.3), custom_call_target="tpu_custom_call" | custom-call | tf_op jit(solution)/shard_map/pallas_call | solution.py:130
  4.3 3.7 %collective-permute-start = (f32[8,104,128]{2,1,0:T(8,128)}, f32[8,104,128]{2,1,0:T(8,128)S(1)}, u32[]{:S(2)}, u32[]{:S(2)}) collective-permute-start(f32[8,104,128]{2,1,0:T(8,128)} %shard_map.56), channel_id=1, source_target_pairs={{0,2},{1,3},{2,0},{3,1},{4,6},{5,7},{6,4},{7,5},{8,10},{9,11},{10,... | collective-permute-start | bytes 1277960 | tf_op jit(solution)/shard_map/ppermute | solution.py:26
  8.0 5.3 %all-to-all-start = ((s32[16,24,128]{2,1,0:T(8,128)}), s32[16,24,128]{2,1,0:T(8,128)S(1)}, u32[]{:S(2)}, u32[]{:S(2)}) async-start(s32[16,24,128]{2,1,0:T(8,128)} %get-tuple-element.28), calls=%async_computation | async-start | bytes 393216 | tf_op jit(solution)/shard_map/all_to_all | solution.py:447
  13.3 4.2 %collective-permute-done = f32[8,104,128]{2,1,0:T(8,128)S(1)} collective-permute-done((f32[8,104,128]{2,1,0:T(8,128)}, f32[8,104,128]{2,1,0:T(8,128)S(1)}, u32[]{:S(2)}, u32[]{:S(2)}) %collective-permute-start) | collective-permute-done | bytes 426016 | tf_op jit(solution)/shard_map/ppermute | solution.py:26
  18.6 3.0 %all-to-all-done = s32[16,24,128]{2,1,0:T(8,128)S(1)} async-done(((s32[16,24,128]{2,1,0:T(8,128)}), s32[16,24,128]{2,1,0:T(8,128)S(1)}, u32[]{:S(2)}, u32[]{:S(2)}) %all-to-all-start) | async-done | bytes 196640 | tf_op jit(solution)/shard_map/all_to_all | solution.py:447
  27.7 3.8 %collective-permute-start.3 = (s32[2,16,24,128]{3,2,1,0:T(8,128)S(1)}, s32[2,16,24,128]{3,2,1,0:T(8,128)S(1)}, u32[]{:S(2)}, u32[]{:S(2)}) collective-permute-start(s32[2,16,24,128]{3,2,1,0:T(8,128)S(1)} %pad_add_fusion.refs_0_), channel_id=1, source_target_pairs={{0,48},{1,49},{2,50},{3,51},{4,52},{5,53},{6,54},{7,55},{8,56},{9,... | collective-permute-start | bytes 1179656 | tf_op jit(solution)/shard_map/ppermute | solution.py:26
  31.5 10.5 %shard_map.57.refs_3_.refs_4_ = bf16[8,512,1024]{2,1,0:T(8,128)(2,1)} custom-call(s32[3]{0:T(128)} %pad_add_fusion.1.where_ref, f32[16384,128]{1,0:T(8,128)} %bitcast.12), custom_call_target="tpu_custom_call" | custom-call | flops 8999999488 | bytes 20971520 | tf_op jit(solution)/shard_map/pallas_call | solution.py:229
  42.1 5.3 %shard_map.58.refs_0_ = s32[2,264,128]{2,1,0:T(8,128)} custom-call(s32[2,16,24,128]{3,2,1,0:T(8,128)} %copy-done.5), custom_call_target="tpu_custom_call" | custom-call | flops 5000000000 | bytes 1048576 | tf_op jit(solution)/shard_map/pallas_call | solution.py:208
  48.7 9.2 %shard_map.59.refs_1_ = s32[4,264,128]{2,1,0:T(8,128)} custom-call(s32[2,16,24,128]{3,2,1,0:T(8,128)} %copy-done.15, s32[2,16,24,128]{3,2,1,0:T(8,128)} %copy-done.14), custom_call_target="tpu_custom_call" | custom-call | flops 10000000000 | bytes 2097152 | tf_op jit(solution)/shard_map/pallas_call | solution.py:208
  57.9 4.6 %collective-permute-done.6.refs_8_.refs_16_ = f32[2,8,104,128]{3,2,1,0:T(8,128)S(1)} collective-permute-done((f32[2,8,104,128]{3,2,1,0:T(8,128)S(1)}, f32[2,8,104,128]{3,2,1,0:T(8,128)S(1)}, u32[]{:S(2)}, u32[]{:S(2)}) %collective-permute-start.6) | collective-permute-done | bytes 852000 | tf_op jit(solution)/shard_map/ppermute | solution.py:26
  66.0 5.3 %shard_map.60.refs_2_ = s32[2,264,128]{2,1,0:T(8,128)} custom-call(s32[2,16,24,128]{3,2,1,0:T(8,128)} %copy-done.13), custom_call_target="tpu_custom_call" | custom-call | flops 5000000000 | bytes 1048576 | tf_op jit(solution)/shard_map/pallas_call | solution.py:208
  73.8 19.7 %shard_map.61 = (f32[256,512]{1,0:T(8,128)}, f32[256,512]{1,0:T(8,128)}) custom-call(s32[3]{0:T(128)} %pad_add_fusion.1.where_ref, s32[2,264,128]{2,1,0:T(8,128)} %shard_map.58.refs_0_, s32[4,264,128]{2,1,0:T(8,128)} %shard_map.59.refs_1_, s32[2,264,128]{2,1,0:T(8,128)} %shard_map.60.refs_2_, bf16[8,512,1024]{2,1,0:T(8,128)(2,1)} %shard_map.57.refs_3_.refs_4_, ...), custom_call_target="tpu_custom_call" | custom-call | flops 17999998976 | bytes 16777216 | tf_op jit(solution)/shard_map/pallas_call | solution.py:365
  103.1 3.4 %collective-permute-done.13 = f32[64,512]{1,0:T(8,128)S(1)} collective-permute-done((f32[64,512]{1,0:T(8,128)S(1)}, f32[64,512]{1,0:T(8,128)S(1)}, u32[]{:S(2)}, u32[]{:S(2)}) %collective-permute-start.13) | collective-permute-done | bytes 131104 | tf_op jit(solution)/shard_map/ppermute | solution.py:26
  108.1 2.4 %collective-permute-start.16 = (f32[64,512]{1,0:T(8,128)S(1)}, f32[64,512]{1,0:T(8,128)S(1)}, u32[]{:S(2)}, u32[]{:S(2)}) collective-permute-start(f32[64,512]{1,0:T(8,128)S(1)} %fusion.1), channel_id=1, source_target_pairs={{0,2},{1,3},{2,0},{3,1},{4,6},{5,7},{6,4},{7,5},{8,10},{9,11},{10,... | collective-permute-start | bytes 393224 | tf_op jit(solution)/shard_map/ppermute | solution.py:26
  111.7 3.1 %collective-permute-done.16 = f32[64,512]{1,0:T(8,128)S(1)} collective-permute-done((f32[64,512]{1,0:T(8,128)S(1)}, f32[64,512]{1,0:T(8,128)S(1)}, u32[]{:S(2)}, u32[]{:S(2)}) %collective-permute-start.16) | collective-permute-done | bytes 131104 | tf_op jit(solution)/shard_map/ppermute | solution.py:26
  114.8 3.8 %collective-permute-start.21 = (f32[64,512]{1,0:T(8,128)S(1)}, f32[64,512]{1,0:T(8,128)S(1)}, u32[]{:S(2)}, u32[]{:S(2)}) collective-permute-start(f32[64,512]{1,0:T(8,128)S(1)} %add_add_fusion.3), channel_id=1, source_target_pairs={{0,48},{1,49},{2,50},{3,51},{4,52},{5,53},{6,54},{7,55},{8,56},{9,... | collective-permute-start | bytes 393224 | tf_op jit(solution)/shard_map/ppermute | solution.py:26
  131.5 5.9 %collective-permute-start.25 = (f32[256,512]{1,0:T(8,128)S(1)}, f32[256,512]{1,0:T(8,128)S(1)}, u32[]{:S(2)}, u32[]{:S(2)}) collective-permute-start(f32[256,512]{1,0:T(8,128)S(1)} %pad_maximum_fusion.1.refs_21_.near_ref), channel_id=1, source_target_pairs={{0,1},{1,0},{2,3},{3,2},{4,5},{5,4},{6,7},{7,6},{8,9},{9,8},{10,11... | collective-permute-start | bytes 1572872 | tf_op jit(solution)/shard_map/ppermute | solution.py:26
  139.7 21.2 %shard_map.62 = (f32[256,512]{1,0:T(8,128)}, f32[256,512]{1,0:T(8,128)}) custom-call(s32[3]{0:T(128)} %pad_add_fusion.1.where_ref, s32[2,264,128]{2,1,0:T(8,128)} %shard_map.58.refs_0_, s32[4,264,128]{2,1,0:T(8,128)} %shard_map.59.refs_1_, s32[2,264,128]{2,1,0:T(8,128)} %shard_map.60.refs_2_, bf16[8,512,1024]{2,1,0:T(8,128)(2,1)} %shard_map.57.refs_3_.refs_4_, ...), custom_call_target="tpu_custom_call" | custom-call | flops 17999998976 | bytes 16777216 | tf_op jit(solution)/shard_map/pallas_call | solution.py:365
  168.3 3.3 %shard_map.63.books_ref = f32[512,2,256]{2,1,0:T(2,128)} custom-call(s32[3]{0:T(128)} %pad_add_fusion.1.where_ref, f32[512,2,256]{2,1,0:T(2,128)} %books_ref.3, f32[256,512]{1,0:T(8,128)} %copy-done, f32[256,512]{1,0:T(8,128)} %copy-done.3), custom_call_target="tpu_custom_call" | custom-call | tf_op jit(solution)/shard_map/pallas_call | solution.py:405
  171.6 2.4 %collective-permute-done.27 = f32[64,512]{1,0:T(8,128)S(1)} collective-permute-done((f32[64,512]{1,0:T(8,128)S(1)}, f32[64,512]{1,0:T(8,128)S(1)}, u32[]{:S(2)}, u32[]{:S(2)}) %collective-permute-start.27) | collective-permute-done | bytes 131104 | tf_op jit(solution)/shard_map/ppermute | solution.py:26
  179.7 2.5 %collective-permute-done.30 = f32[64,512]{1,0:T(8,128)S(1)} collective-permute-done((f32[64,512]{1,0:T(8,128)S(1)}, f32[64,512]{1,0:T(8,128)S(1)}, u32[]{:S(2)}, u32[]{:S(2)}) %collective-permute-start.30) | collective-permute-done | bytes 131104 | tf_op jit(solution)/shard_map/ppermute | solution.py:26
  182.3 2.4 %collective-permute-start.35 = (f32[64,512]{1,0:T(8,128)S(1)}, f32[64,512]{1,0:T(8,128)S(1)}, u32[]{:S(2)}, u32[]{:S(2)}) collective-permute-start(f32[64,512]{1,0:T(8,128)S(1)} %add_add_fusion.1), channel_id=1, source_target_pairs={{0,48},{1,49},{2,50},{3,51},{4,52},{5,53},{6,54},{7,55},{8,56},{9,... | collective-permute-start | bytes 393224 | tf_op jit(solution)/shard_map/ppermute | solution.py:26
  197.2 5.8 %collective-permute-start.39 = (f32[256,512]{1,0:T(8,128)S(1)}, f32[256,512]{1,0:T(8,128)S(1)}, u32[]{:S(2)}, u32[]{:S(2)}) collective-permute-start(f32[256,512]{1,0:T(8,128)S(1)} %pad_maximum_fusion.2.near_ref), channel_id=1, source_target_pairs={{0,1},{1,0},{2,3},{3,2},{4,5},{5,4},{6,7},{7,6},{8,9},{9,8},{10,11... | collective-permute-start | bytes 1572872 | tf_op jit(solution)/shard_map/ppermute | solution.py:26
  205.4 3.2 %shard_map.64 = f32[512,2,256]{2,1,0:T(2,128)} custom-call(s32[3]{0:T(128)} %pad_add_fusion.1.where_ref, f32[512,2,256]{2,1,0:T(2,128)} %shard_map.63.books_ref, f32[256,512]{1,0:T(8,128)} %copy-done.1, f32[256,512]{1,0:T(8,128)} %copy-done.4), custom_call_target="tpu_custom_call" | custom-call | tf_op jit(solution)/shard_map/pallas_call | solution.py:405
  (115 shorter events, 71.8 us)
Async XLA Ops:
  4.3 13.2 %collective-permute-start = (f32[8,104,128]{2,1,0:T(8,128)}, f32[8,104,128]{2,1,0:T(8,128)S(1)}, u32[]{:S(2)}, u32[]{:S(2)}) collective-permute-start(f32[8,104,128]{2,1,0:T(8,128)} %shard_map.56), channel_id=1, source_target_pairs={{0,2},{1,3},{2,0},{3,1},{4,6},{5,7},{6,4},{7,5},{8,10},{9,11},{10,... | collective-permute-start | bytes 1277960 | tf_op jit(solution)/shard_map/ppermute | solution.py:26
  8.0 13.6 %all-to-all-start = ((s32[16,24,128]{2,1,0:T(8,128)}), s32[16,24,128]{2,1,0:T(8,128)S(1)}, u32[]{:S(2)}, u32[]{:S(2)}) async-start(s32[16,24,128]{2,1,0:T(8,128)} %get-tuple-element.28), calls=%async_computation | async-start | bytes 393216 | tf_op jit(solution)/shard_map/all_to_all | solution.py:447
  21.6 6.1 %collective-permute-start.1 = (s32[16,24,128]{2,1,0:T(8,128)S(1)}, s32[16,24,128]{2,1,0:T(8,128)S(1)}, u32[]{:S(2)}, u32[]{:S(2)}) collective-permute-start(s32[16,24,128]{2,1,0:T(8,128)S(1)} %all-to-all-done), channel_id=1, source_target_pairs={{0,64},{1,65},{2,66},{3,67},{4,68},{5,69},{6,70},{7,71},{8,72},{9,... | collective-permute-start | bytes 589832 | tf_op jit(solution)/shard_map/ppermute | solution.py:26
  23.2 39.3 %collective-permute-start.6 = (f32[2,8,104,128]{3,2,1,0:T(8,128)S(1)}, f32[2,8,104,128]{3,2,1,0:T(8,128)S(1)}, u32[]{:S(2)}, u32[]{:S(2)}) collective-permute-start(f32[2,8,104,128]{3,2,1,0:T(8,128)S(1)} %pad_maximum_fusion.refs_5_.refs_13_), channel_id=1, source_target_pairs={{0,12},{1,13},{2,14},{3,15},{4,8},{5,9},{6,10},{7,11},{8,4},{9,5},... | collective-permute-start | bytes 2555912 | tf_op jit(solution)/shard_map/ppermute | solution.py:26
  25.0 37.5 %collective-permute-start.5 = (f32[2,8,104,128]{3,2,1,0:T(8,128)S(1)}, f32[2,8,104,128]{3,2,1,0:T(8,128)S(1)}, u32[]{:S(2)}, u32[]{:S(2)}) collective-permute-start(f32[2,8,104,128]{3,2,1,0:T(8,128)S(1)} %pad_maximum_fusion.refs_5_.refs_13_), channel_id=1, source_target_pairs={{0,8},{1,9},{2,10},{3,11},{4,12},{5,13},{6,14},{7,15},{8,0},{9,1},... | collective-permute-start | bytes 2555912 | tf_op jit(solution)/shard_map/ppermute | solution.py:26
  25.5 37.3 %collective-permute-start.4 = (f32[2,8,104,128]{3,2,1,0:T(8,128)S(1)}, f32[2,8,104,128]{3,2,1,0:T(8,128)S(1)}, u32[]{:S(2)}, u32[]{:S(2)}) collective-permute-start(f32[2,8,104,128]{3,2,1,0:T(8,128)S(1)} %pad_maximum_fusion.refs_5_.refs_13_), channel_id=1, source_target_pairs={{0,4},{1,5},{2,6},{3,7},{4,0},{5,1},{6,2},{7,3},{8,12},{9,13},{10,... | collective-permute-start | bytes 2555912 | tf_op jit(solution)/shard_map/ppermute | solution.py:26
  27.7 19.7 %collective-permute-start.3 = (s32[2,16,24,128]{3,2,1,0:T(8,128)S(1)}, s32[2,16,24,128]{3,2,1,0:T(8,128)S(1)}, u32[]{:S(2)}, u32[]{:S(2)}) collective-permute-start(s32[2,16,24,128]{3,2,1,0:T(8,128)S(1)} %pad_add_fusion.refs_0_), channel_id=1, source_target_pairs={{0,48},{1,49},{2,50},{3,51},{4,52},{5,53},{6,54},{7,55},{8,56},{9,... | collective-permute-start | bytes 1179656 | tf_op jit(solution)/shard_map/ppermute | solution.py:26
  31.5 15.8 %collective-permute-start.2 = (s32[2,16,24,128]{3,2,1,0:T(8,128)S(1)}, s32[2,16,24,128]{3,2,1,0:T(8,128)S(1)}, u32[]{:S(2)}, u32[]{:S(2)}) collective-permute-start(s32[2,16,24,128]{3,2,1,0:T(8,128)S(1)} %pad_add_fusion.refs_0_), channel_id=1, source_target_pairs={{0,16},{1,17},{2,18},{3,19},{4,20},{5,21},{6,22},{7,23},{8,24},{9,... | collective-permute-start | bytes 1179656 | tf_op jit(solution)/shard_map/ppermute | solution.py:26
  47.4 17.9 %collective-permute-start.7 = (s32[2,16,24,128]{3,2,1,0:T(8,128)}, s32[2,16,24,128]{3,2,1,0:T(8,128)S(1)}, u32[]{:S(2)}, u32[]{:S(2)}) collective-permute-start(s32[2,16,24,128]{3,2,1,0:T(8,128)} %copy-done.5), channel_id=1, source_target_pairs={{0,32},{1,33},{2,34},{3,35},{4,36},{5,37},{6,38},{7,39},{8,40},{9,... | collective-permute-start | bytes 1179656 | tf_op jit(solution)/shard_map/ppermute | solution.py:26
  62.9 8.5 %collective-permute-start.8 = (f32[2,8,104,128]{3,2,1,0:T(8,128)S(1)}, f32[2,8,104,128]{3,2,1,0:T(8,128)S(1)}, u32[]{:S(2)}, u32[]{:S(2)}) collective-permute-start(f32[2,8,104,128]{3,2,1,0:T(8,128)S(1)} %pad_maximum_fusion.refs_5_.refs_13_), channel_id=1, source_target_pairs={{0,1},{1,0},{2,3},{3,2},{4,5},{5,4},{6,7},{7,6},{8,9},{9,8},{10,11... | collective-permute-start | bytes 2555912 | tf_op jit(solution)/shard_map/ppermute | solution.py:26
  64.7 6.7 %collective-permute-start.9 = (f32[2,8,104,128]{3,2,1,0:T(8,128)S(1)}, f32[2,8,104,128]{3,2,1,0:T(8,128)S(1)}, u32[]{:S(2)}, u32[]{:S(2)}) collective-permute-start(f32[2,8,104,128]{3,2,1,0:T(8,128)S(1)} %collective-permute-done.4.refs_6_.refs_14_), channel_id=1, source_target_pairs={{0,1},{1,0},{2,3},{3,2},{4,5},{5,4},{6,7},{7,6},{8,9},{9,8},{10,11... | collective-permute-start | bytes 2555912 | tf_op jit(solution)/shard_map/ppermute | solution.py:26
  64.8 6.6 %collective-permute-start.10 = (f32[2,8,104,128]{3,2,1,0:T(8,128)S(1)}, f32[2,8,104,128]{3,2,1,0:T(8,128)S(1)}, u32[]{:S(2)}, u32[]{:S(2)}) collective-permute-start(f32[2,8,104,128]{3,2,1,0:T(8,128)S(1)} %collective-permute-done.5.refs_7_.refs_15_), channel_id=1, source_target_pairs={{0,1},{1,0},{2,3},{3,2},{4,5},{5,4},{6,7},{7,6},{8,9},{9,8},{10,11... | collective-permute-start | bytes 2555912 | tf_op jit(solution)/shard_map/ppermute | solution.py:26
  65.2 6.2 %collective-permute-start.11 = (f32[2,8,104,128]{3,2,1,0:T(8,128)S(1)}, f32[2,8,104,128]{3,2,1,0:T(8,128)S(1)}, u32[]{:S(2)}, u32[]{:S(2)}) collective-permute-start(f32[2,8,104,128]{3,2,1,0:T(8,128)S(1)} %collective-permute-done.6.refs_8_.refs_16_), channel_id=1, source_target_pairs={{0,1},{1,0},{2,3},{3,2},{4,5},{5,4},{6,7},{7,6},{8,9},{9,8},{10,11... | collective-permute-start | bytes 2555912 | tf_op jit(solution)/shard_map/ppermute | solution.py:26
  96.9 6.0 %collective-permute-start.15 = (f32[64,512]{1,0:T(8,128)S(1)}, f32[64,512]{1,0:T(8,128)S(1)}, u32[]{:S(2)}, u32[]{:S(2)}) collective-permute-start(f32[64,512]{1,0:T(8,128)S(1)} %get-tuple-element.54), channel_id=1, source_target_pairs={{0,12},{1,13},{2,14},{3,15},{4,8},{5,9},{6,10},{7,11},{8,4},{9,5},... | collective-permute-start | bytes 393224 | tf_op jit(solution)/shard_map/ppermute | solution.py:26
  98.7 7.8 %collective-permute-start.13 = (f32[64,512]{1,0:T(8,128)S(1)}, f32[64,512]{1,0:T(8,128)S(1)}, u32[]{:S(2)}, u32[]{:S(2)}) collective-permute-start(f32[64,512]{1,0:T(8,128)S(1)} %get-tuple-element.56), channel_id=1, source_target_pairs={{0,8},{1,9},{2,10},{3,11},{4,12},{5,13},{6,14},{7,15},{8,0},{9,1},... | collective-permute-start | bytes 393224 | tf_op jit(solution)/shard_map/ppermute | solution.py:26
  108.1 6.6 %collective-permute-start.16 = (f32[64,512]{1,0:T(8,128)S(1)}, f32[64,512]{1,0:T(8,128)S(1)}, u32[]{:S(2)}, u32[]{:S(2)}) collective-permute-start(f32[64,512]{1,0:T(8,128)S(1)} %fusion.1), channel_id=1, source_target_pairs={{0,2},{1,3},{2,0},{3,1},{4,6},{5,7},{6,4},{7,5},{8,10},{9,11},{10,... | collective-permute-start | bytes 393224 | tf_op jit(solution)/shard_map/ppermute | solution.py:26
  114.8 6.2 %collective-permute-start.21 = (f32[64,512]{1,0:T(8,128)S(1)}, f32[64,512]{1,0:T(8,128)S(1)}, u32[]{:S(2)}, u32[]{:S(2)}) collective-permute-start(f32[64,512]{1,0:T(8,128)S(1)} %add_add_fusion.3), channel_id=1, source_target_pairs={{0,48},{1,49},{2,50},{3,51},{4,52},{5,53},{6,54},{7,55},{8,56},{9,... | collective-permute-start | bytes 393224 | tf_op jit(solution)/shard_map/ppermute | solution.py:26
  118.6 5.4 %collective-permute-start.19 = (f32[64,512]{1,0:T(8,128)S(1)}, f32[64,512]{1,0:T(8,128)S(1)}, u32[]{:S(2)}, u32[]{:S(2)}) collective-permute-start(f32[64,512]{1,0:T(8,128)S(1)} %add_add_fusion.3), channel_id=1, source_target_pairs={{0,32},{1,33},{2,34},{3,35},{4,36},{5,37},{6,38},{7,39},{8,40},{9,... | collective-permute-start | bytes 393224 | tf_op jit(solution)/shard_map/ppermute | solution.py:26
  131.5 7.4 %collective-permute-start.25 = (f32[256,512]{1,0:T(8,128)S(1)}, f32[256,512]{1,0:T(8,128)S(1)}, u32[]{:S(2)}, u32[]{:S(2)}) collective-permute-start(f32[256,512]{1,0:T(8,128)S(1)} %pad_maximum_fusion.1.refs_21_.near_ref), channel_id=1, source_target_pairs={{0,1},{1,0},{2,3},{3,2},{4,5},{5,4},{6,7},{7,6},{8,9},{9,8},{10,11... | collective-permute-start | bytes 1572872 | tf_op jit(solution)/shard_map/ppermute | solution.py:26
  164.3 7.3 %collective-permute-start.29 = (f32[64,512]{1,0:T(8,128)S(1)}, f32[64,512]{1,0:T(8,128)S(1)}, u32[]{:S(2)}, u32[]{:S(2)}) collective-permute-start(f32[64,512]{1,0:T(8,128)S(1)} %get-tuple-element.51), channel_id=1, source_target_pairs={{0,12},{1,13},{2,14},{3,15},{4,8},{5,9},{6,10},{7,11},{8,4},{9,5},... | collective-permute-start | bytes 393224 | tf_op jit(solution)/shard_map/ppermute | solution.py:26
  166.1 5.5 %collective-permute-start.28 = (f32[64,512]{1,0:T(8,128)S(1)}, f32[64,512]{1,0:T(8,128)S(1)}, u32[]{:S(2)}, u32[]{:S(2)}) collective-permute-start(f32[64,512]{1,0:T(8,128)S(1)} %get-tuple-element.52), channel_id=1, source_target_pairs={{0,4},{1,5},{2,6},{3,7},{4,0},{5,1},{6,2},{7,3},{8,12},{9,13},{10,... | collective-permute-start | bytes 393224 | tf_op jit(solution)/shard_map/ppermute | solution.py:26
  166.1 7.9 %collective-permute-start.27 = (f32[64,512]{1,0:T(8,128)S(1)}, f32[64,512]{1,0:T(8,128)S(1)}, u32[]{:S(2)}, u32[]{:S(2)}) collective-permute-start(f32[64,512]{1,0:T(8,128)S(1)} %get-tuple-element.53), channel_id=1, source_target_pairs={{0,8},{1,9},{2,10},{3,11},{4,12},{5,13},{6,14},{7,15},{8,0},{9,1},... | collective-permute-start | bytes 393224 | tf_op jit(solution)/shard_map/ppermute | solution.py:26
  175.9 6.3 %collective-permute-start.30 = (f32[64,512]{1,0:T(8,128)S(1)}, f32[64,512]{1,0:T(8,128)S(1)}, u32[]{:S(2)}, u32[]{:S(2)}) collective-permute-start(f32[64,512]{1,0:T(8,128)S(1)} %fusion), channel_id=1, source_target_pairs={{0,2},{1,3},{2,0},{3,1},{4,6},{5,7},{6,4},{7,5},{8,10},{9,11},{10,... | collective-permute-start | bytes 393224 | tf_op jit(solution)/shard_map/ppermute | solution.py:26
  197.2 7.4 %collective-permute-start.39 = (f32[256,512]{1,0:T(8,128)S(1)}, f32[256,512]{1,0:T(8,128)S(1)}, u32[]{:S(2)}, u32[]{:S(2)}) collective-permute-start(f32[256,512]{1,0:T(8,128)S(1)} %pad_maximum_fusion.2.near_ref), channel_id=1, source_target_pairs={{0,1},{1,0},{2,3},{3,2},{4,5},{5,4},{6,7},{7,6},{8,9},{9,8},{10,11... | collective-permute-start | bytes 1572872 | tf_op jit(solution)/shard_map/ppermute | solution.py:26
  (33 other events, 186.0 us)

commit v3 on v2

--- a/solution.py
+++ b/solution.py
@@ -74,7 +74,7 @@
     return pl.ds(start + tile * 16 + parity, 8, stride=2)
 
 
-def pieces_kernel(tile_ref, codes_ref, piece_ref, own_ref, held_ref):
+def make_pieces(tile_ref, codes_ref, piece_ref, own_ref, held_ref):
     lane = iota((8, 128), 1)
     left = lane < 64
     for q in range(8):
@@ -96,17 +96,8 @@
             piece_ref[2 * q + h, 16:24, :] = books
 
 
-def make_pieces(codes, tile_map):
-    return pl.pallas_call(
-        pieces_kernel,
-        out_shape=[jax.ShapeDtypeStruct((16, 24, 128), I32), jax.ShapeDtypeStruct((32, 1024), I32)],
-        in_specs=[in_smem()] + in_vmem(1),
-        out_specs=in_vmem(2),
-        scratch_shapes=[pltpu.VMEM((256, 128), I32)],
-    )(tile_map, codes)
-
-
-def first_kernel(tile_ref, weights_ref, own_ref, books_ref, out_ref, weight_ref):
+def first_kernel(tile_ref, weights_ref, codes_ref, books_ref, out_ref, piece_ref, weight_ref, own_ref, held_ref):
+    make_pieces(tile_ref, codes_ref, piece_ref, own_ref, held_ref)
     parting = part_pairs()
     for q in range(8):
         parted = dot_nn(weights_ref[:, q * 256 : q * 256 + 256], parting)
@@ -126,14 +117,14 @@
         out_ref[q, 96:104, :] = jnp.where(iota((8, 128), 0) == 0, tile_ref[0, q], tile_ref[1, q]).astype(F32)
 
 
-def first(weights, own, tile_map, codebooks):
+def first(weights, codes, tile_map, codebooks):
     return pl.pallas_call(
         first_kernel,
-        out_shape=jax.ShapeDtypeStruct((8, 104, 128), F32),
+        out_shape=[jax.ShapeDtypeStruct((8, 104, 128), F32), jax.ShapeDtypeStruct((16, 24, 128), I32)],
         in_specs=[in_smem()] + in_vmem(3),
-        out_specs=in_vmem(1)[0],
-        scratch_shapes=[pltpu.VMEM((512, 128), F32)],
-    )(tile_map, weights, own, codebooks)
+        out_specs=in_vmem(2),
+        scratch_shapes=[pltpu.VMEM((512, 128), F32), pltpu.VMEM((32, 1024), I32), pltpu.VMEM((256, 128), I32)],
+    )(tile_map, weights, codes, codebooks)
 
 
 def spot(position):
@@ -443,9 +434,9 @@
 def per_device(hessian, weights, codes, tile_map, codebooks):
     row, col = lax.axis_index("row").astype(I32), lax.axis_index("col").astype(I32)
     where = jnp.stack([row, col, (col & 1) * 256 + (col >> 2) * 64])
-    pieces, own = make_pieces(codes, tile_map)
+    mine, pieces = first(weights, codes, tile_map, codebooks)
     pieces = lax.all_to_all(pieces, "col", 0, 0, tiled=True)
-    pair = pair_up(first(weights, own, tile_map, codebooks))
+    pair = pair_up(mine)
     pieces, pair = hold(pieces, pair)
 
     around = over_x(pair)

time: 209 us -> 208 us (level)
    pallas_call x2 -> x1, Pallas kernels: 4.27 us -> 2.59 us  [first(): pl.pallas_call(first_kernel, out_shape=[jax.ShapeDtypeStruct((8, 104, 128...]
where the time goes in v3:
time: 208 us; the launch traced here: 207 us
  Pallas kernels  80.3 us (39%)
  starting transfers between devices  65.3 us (31%)
  waiting for transfers between devices  52.2 us (25%)
  local copies, waits for them, and re-layouts  4.85 us (2%)
  other arithmetic  4.22 us (2%)
    ppermute x40, starting transfers between devices, swap(): return lax.ppermute(v, BOTH, partners(dx, dyh, dcore, dyl, dz))  60 us
    ppermute x40, waiting for transfers between devices, swap(): return lax.ppermute(v, BOTH, partners(dx, dyh, dcore, dyl, dz))  49.1 us
    pallas_call x2, Pallas kernels, step(): pl.pallas_call(kernel, out_shape=[half, half], grid=(5,), in_specs=[in_sm...  40.9 us
    pallas_call x3, Pallas kernels, sort_codes(): pl.pallas_call(sort_kernel, out_shape=jax.ShapeDtypeStruct((2 * many, 264...  19.7 us
    pallas_call x1, Pallas kernels, split_hessian(): pl.pallas_call(split_kernel, out_shape=jax.ShapeDtypeStruct((8, 512, 1024...  10.5 us
    pallas_call x2, Pallas kernels, update(): pl.pallas_call(update_kernel, out_shape=jax.ShapeDtypeStruct((512, 2, 256...  6.55 us
    all_to_all x1, starting transfers between devices, per_device(): pieces = lax.all_to_all(pieces, 'col', 0, 0, tiled=True)  5.27 us
    unnamed x32, local copies, waits for them, and re-layouts  4.79 us
  transfers between devices with their start and end apart: 41, of which 29 were waited for; matrix products, arithmetic and copies ran while one was open for 1% of the time, Pallas kernels for 16%

profile of v3, /device:TPU:1, one launch (start us, length us, event | category | flops | bytes accessed | tf_op | source)
XLA Modules:
  0.0 207.0 jit_solution(310503898998137984)
XLA Ops:
  0.0 2.6 %shard_map.55 = (f32[8,104,128]{2,1,0:T(8,128)}, s32[16,24,128]{2,1,0:T(8,128)}) custom-call(s32[2,8]{1,0:T(2,128)} %tile_ref.1, bf16[32,2048]{1,0:T(8,128)(2,1)} %weights_ref.1, s32[32,1024]{1,0:T(8,128)} %codes_ref.1, f32[512,2,256]{2,1,0:T(2,128)} %books_ref.3), custom_call_target="tpu_custom_call" | custom-call | tf_op jit(solution)/shard_map/pallas_call | solution.py:121
  2.6 3.7 %collective-permute-start = (f32[8,104,128]{2,1,0:T(8,128)}, f32[8,104,128]{2,1,0:T(8,128)S(1)}, u32[]{:S(2)}, u32[]{:S(2)}) collective-permute-start(f32[8,104,128]{2,1,0:T(8,128)} %get-tuple-element.29), channel_id=1, source_target_pairs={{0,2},{1,3},{2,0},{3,1},{4,6},{5,7},{6,4},{7,5},{8,10},{9,11},{10,... | collective-permute-start | bytes 1277960 | tf_op jit(solution)/shard_map/ppermute | solution.py:26
  6.3 5.3 %all-to-all-start = ((s32[16,24,128]{2,1,0:T(8,128)}), s32[16,24,128]{2,1,0:T(8,128)S(1)}, u32[]{:S(2)}, u32[]{:S(2)}) async-start(s32[16,24,128]{2,1,0:T(8,128)} %get-tuple-element.28), calls=%async_computation | async-start | bytes 393216 | tf_op jit(solution)/shard_map/all_to_all | solution.py:438
  11.6 4.2 %collective-permute-done = f32[8,104,128]{2,1,0:T(8,128)S(1)} collective-permute-done((f32[8,104,128]{2,1,0:T(8,128)}, f32[8,104,128]{2,1,0:T(8,128)S(1)}, u32[]{:S(2)}, u32[]{:S(2)}) %collective-permute-start) | collective-permute-done | bytes 426016 | tf_op jit(solution)/shard_map/ppermute | solution.py:26
  16.9 3.0 %all-to-all-done = s32[16,24,128]{2,1,0:T(8,128)S(1)} async-done(((s32[16,24,128]{2,1,0:T(8,128)}), s32[16,24,128]{2,1,0:T(8,128)S(1)}, u32[]{:S(2)}, u32[]{:S(2)}) %all-to-all-start) | async-done | bytes 196640 | tf_op jit(solution)/shard_map/all_to_all | solution.py:438
  26.0 3.8 %collective-permute-start.3 = (s32[2,16,24,128]{3,2,1,0:T(8,128)S(1)}, s32[2,16,24,128]{3,2,1,0:T(8,128)S(1)}, u32[]{:S(2)}, u32[]{:S(2)}) collective-permute-start(s32[2,16,24,128]{3,2,1,0:T(8,128)S(1)} %pad_add_fusion.refs_0_), channel_id=1, source_target_pairs={{0,48},{1,49},{2,50},{3,51},{4,52},{5,53},{6,54},{7,55},{8,56},{9,... | collective-permute-start | bytes 1179656 | tf_op jit(solution)/shard_map/ppermute | solution.py:26
  29.9 10.5 %shard_map.56.refs_3_.refs_4_ = bf16[8,512,1024]{2,1,0:T(8,128)(2,1)} custom-call(s32[3]{0:T(128)} %pad_add_fusion.1.where_ref, f32[16384,128]{1,0:T(8,128)} %bitcast.12), custom_call_target="tpu_custom_call" | custom-call | flops 8999999488 | bytes 20971520 | tf_op jit(solution)/shard_map/pallas_call | solution.py:220
  40.4 5.3 %shard_map.57.refs_0_ = s32[2,264,128]{2,1,0:T(8,128)} custom-call(s32[2,16,24,128]{3,2,1,0:T(8,128)} %copy-done.5), custom_call_target="tpu_custom_call" | custom-call | flops 5000000000 | bytes 1048576 | tf_op jit(solution)/shard_map/pallas_call | solution.py:199
  47.0 9.2 %shard_map.58.refs_1_ = s32[4,264,128]{2,1,0:T(8,128)} custom-call(s32[2,16,24,128]{3,2,1,0:T(8,128)} %copy-done.15, s32[2,16,24,128]{3,2,1,0:T(8,128)} %copy-done.14), custom_call_target="tpu_custom_call" | custom-call | flops 10000000000 | bytes 2097152 | tf_op jit(solution)/shard_map/pallas_call | solution.py:199
  56.2 4.6 %collective-permute-done.6.refs_8_.refs_16_ = f32[2,8,104,128]{3,2,1,0:T(8,128)S(1)} collective-permute-done((f32[2,8,104,128]{3,2,1,0:T(8,128)S(1)}, f32[2,8,104,128]{3,2,1,0:T(8,128)S(1)}, u32[]{:S(2)}, u32[]{:S(2)}) %collective-permute-start.6) | collective-permute-done | bytes 852000 | tf_op jit(solution)/shard_map/ppermute | solution.py:26
  64.4 5.3 %shard_map.59.refs_2_ = s32[2,264,128]{2,1,0:T(8,128)} custom-call(s32[2,16,24,128]{3,2,1,0:T(8,128)} %copy-done.13), custom_call_target="tpu_custom_call" | custom-call | flops 5000000000 | bytes 1048576 | tf_op jit(solution)/shard_map/pallas_call | solution.py:199
  72.1 19.7 %shard_map.60 = (f32[256,512]{1,0:T(8,128)}, f32[256,512]{1,0:T(8,128)}) custom-call(s32[3]{0:T(128)} %pad_add_fusion.1.where_ref, s32[2,264,128]{2,1,0:T(8,128)} %shard_map.57.refs_0_, s32[4,264,128]{2,1,0:T(8,128)} %shard_map.58.refs_1_, s32[2,264,128]{2,1,0:T(8,128)} %shard_map.59.refs_2_, bf16[8,512,1024]{2,1,0:T(8,128)(2,1)} %shard_map.56.refs_3_.refs_4_, ...), custom_call_target="tpu_custom_call" | custom-call | flops 17999998976 | bytes 16777216 | tf_op jit(solution)/shard_map/pallas_call | solution.py:356
  101.4 3.4 %collective-permute-done.13 = f32[64,512]{1,0:T(8,128)S(1)} collective-permute-done((f32[64,512]{1,0:T(8,128)S(1)}, f32[64,512]{1,0:T(8,128)S(1)}, u32[]{:S(2)}, u32[]{:S(2)}) %collective-permute-start.13) | collective-permute-done | bytes 131104 | tf_op jit(solution)/shard_map/ppermute | solution.py:26
  106.4 2.4 %collective-permute-start.16 = (f32[64,512]{1,0:T(8,128)S(1)}, f32[64,512]{1,0:T(8,128)S(1)}, u32[]{:S(2)}, u32[]{:S(2)}) collective-permute-start(f32[64,512]{1,0:T(8,128)S(1)} %fusion.1), channel_id=1, source_target_pairs={{0,2},{1,3},{2,0},{3,1},{4,6},{5,7},{6,4},{7,5},{8,10},{9,11},{10,... | collective-permute-start | bytes 393224 | tf_op jit(solution)/shard_map/ppermute | solution.py:26
  110.0 3.1 %collective-permute-done.16 = f32[64,512]{1,0:T(8,128)S(1)} collective-permute-done((f32[64,512]{1,0:T(8,128)S(1)}, f32[64,512]{1,0:T(8,128)S(1)}, u32[]{:S(2)}, u32[]{:S(2)}) %collective-permute-start.16) | collective-permute-done | bytes 131104 | tf_op jit(solution)/shard_map/ppermute | solution.py:26
  113.1 3.8 %collective-permute-start.21 = (f32[64,512]{1,0:T(8,128)S(1)}, f32[64,512]{1,0:T(8,128)S(1)}, u32[]{:S(2)}, u32[]{:S(2)}) collective-permute-start(f32[64,512]{1,0:T(8,128)S(1)} %add_add_fusion.3), channel_id=1, source_target_pairs={{0,48},{1,49},{2,50},{3,51},{4,52},{5,53},{6,54},{7,55},{8,56},{9,... | collective-permute-start | bytes 393224 | tf_op jit(solution)/shard_map/ppermute | solution.py:26
  129.9 5.9 %collective-permute-start.25 = (f32[256,512]{1,0:T(8,128)S(1)}, f32[256,512]{1,0:T(8,128)S(1)}, u32[]{:S(2)}, u32[]{:S(2)}) collective-permute-start(f32[256,512]{1,0:T(8,128)S(1)} %pad_maximum_fusion.1.refs_21_.near_ref), channel_id=1, source_target_pairs={{0,1},{1,0},{2,3},{3,2},{4,5},{5,4},{6,7},{7,6},{8,9},{9,8},{10,11... | collective-permute-start | bytes 1572872 | tf_op jit(solution)/shard_map/ppermute | solution.py:26
  138.1 21.2 %shard_map.61 = (f32[256,512]{1,0:T(8,128)}, f32[256,512]{1,0:T(8,128)}) custom-call(s32[3]{0:T(128)} %pad_add_fusion.1.where_ref, s32[2,264,128]{2,1,0:T(8,128)} %shard_map.57.refs_0_, s32[4,264,128]{2,1,0:T(8,128)} %shard_map.58.refs_1_, s32[2,264,128]{2,1,0:T(8,128)} %shard_map.59.refs_2_, bf16[8,512,1024]{2,1,0:T(8,128)(2,1)} %shard_map.56.refs_3_.refs_4_, ...), custom_call_target="tpu_custom_call" | custom-call | flops 17999998976 | bytes 16777216 | tf_op jit(solution)/shard_map/pallas_call | solution.py:356
  166.6 3.3 %shard_map.62.books_ref = f32[512,2,256]{2,1,0:T(2,128)} custom-call(s32[3]{0:T(128)} %pad_add_fusion.1.where_ref, f32[512,2,256]{2,1,0:T(2,128)} %books_ref.3, f32[256,512]{1,0:T(8,128)} %copy-done, f32[256,512]{1,0:T(8,128)} %copy-done.3), custom_call_target="tpu_custom_call" | custom-call | tf_op jit(solution)/shard_map/pallas_call | solution.py:396
  169.9 2.4 %collective-permute-done.27 = f32[64,512]{1,0:T(8,128)S(1)} collective-permute-done((f32[64,512]{1,0:T(8,128)S(1)}, f32[64,512]{1,0:T(8,128)S(1)}, u32[]{:S(2)}, u32[]{:S(2)}) %collective-permute-start.27) | collective-permute-done | bytes 131104 | tf_op jit(solution)/shard_map/ppermute | solution.py:26
  178.0 2.5 %collective-permute-done.30 = f32[64,512]{1,0:T(8,128)S(1)} collective-permute-done((f32[64,512]{1,0:T(8,128)S(1)}, f32[64,512]{1,0:T(8,128)S(1)}, u32[]{:S(2)}, u32[]{:S(2)}) %collective-permute-start.30) | collective-permute-done | bytes 131104 | tf_op jit(solution)/shard_map/ppermute | solution.py:26
  180.6 2.4 %collective-permute-start.35 = (f32[64,512]{1,0:T(8,128)S(1)}, f32[64,512]{1,0:T(8,128)S(1)}, u32[]{:S(2)}, u32[]{:S(2)}) collective-permute-start(f32[64,512]{1,0:T(8,128)S(1)} %add_add_fusion.1), channel_id=1, source_target_pairs={{0,48},{1,49},{2,50},{3,51},{4,52},{5,53},{6,54},{7,55},{8,56},{9,... | collective-permute-start | bytes 393224 | tf_op jit(solution)/shard_map/ppermute | solution.py:26
  195.6 5.8 %collective-permute-start.39 = (f32[256,512]{1,0:T(8,128)S(1)}, f32[256,512]{1,0:T(8,128)S(1)}, u32[]{:S(2)}, u32[]{:S(2)}) collective-permute-start(f32[256,512]{1,0:T(8,128)S(1)} %pad_maximum_fusion.2.near_ref), channel_id=1, source_target_pairs={{0,1},{1,0},{2,3},{3,2},{4,5},{5,4},{6,7},{7,6},{8,9},{9,8},{10,11... | collective-permute-start | bytes 1572872 | tf_op jit(solution)/shard_map/ppermute | solution.py:26
  203.8 3.2 %shard_map.63 = f32[512,2,256]{2,1,0:T(2,128)} custom-call(s32[3]{0:T(128)} %pad_add_fusion.1.where_ref, f32[512,2,256]{2,1,0:T(2,128)} %shard_map.62.books_ref, f32[256,512]{1,0:T(8,128)} %copy-done.1, f32[256,512]{1,0:T(8,128)} %copy-done.4), custom_call_target="tpu_custom_call" | custom-call | tf_op jit(solution)/shard_map/pallas_call | solution.py:396
  (114 shorter events, 70.1 us)
Async XLA Ops:
  2.6 13.2 %collective-permute-start = (f32[8,104,128]{2,1,0:T(8,128)}, f32[8,104,128]{2,1,0:T(8,128)S(1)}, u32[]{:S(2)}, u32[]{:S(2)}) collective-permute-start(f32[8,104,128]{2,1,0:T(8,128)} %get-tuple-element.29), channel_id=1, source_target_pairs={{0,2},{1,3},{2,0},{3,1},{4,6},{5,7},{6,4},{7,5},{8,10},{9,11},{10,... | collective-permute-start | bytes 1277960 | tf_op jit(solution)/shard_map/ppermute | solution.py:26
  6.3 13.6 %all-to-all-start = ((s32[16,24,128]{2,1,0:T(8,128)}), s32[16,24,128]{2,1,0:T(8,128)S(1)}, u32[]{:S(2)}, u32[]{:S(2)}) async-start(s32[16,24,128]{2,1,0:T(8,128)} %get-tuple-element.28), calls=%async_computation | async-start | bytes 393216 | tf_op jit(solution)/shard_map/all_to_all | solution.py:438
  19.9 6.1 %collective-permute-start.1 = (s32[16,24,128]{2,1,0:T(8,128)S(1)}, s32[16,24,128]{2,1,0:T(8,128)S(1)}, u32[]{:S(2)}, u32[]{:S(2)}) collective-permute-start(s32[16,24,128]{2,1,0:T(8,128)S(1)} %all-to-all-done), channel_id=1, source_target_pairs={{0,64},{1,65},{2,66},{3,67},{4,68},{5,69},{6,70},{7,71},{8,72},{9,... | collective-permute-start | bytes 589832 | tf_op jit(solution)/shard_map/ppermute | solution.py:26
  21.6 39.3 %collective-permute-start.6 = (f32[2,8,104,128]{3,2,1,0:T(8,128)S(1)}, f32[2,8,104,128]{3,2,1,0:T(8,128)S(1)}, u32[]{:S(2)}, u32[]{:S(2)}) collective-permute-start(f32[2,8,104,128]{3,2,1,0:T(8,128)S(1)} %pad_maximum_fusion.refs_5_.refs_13_), channel_id=1, source_target_pairs={{0,12},{1,13},{2,14},{3,15},{4,8},{5,9},{6,10},{7,11},{8,4},{9,5},... | collective-permute-start | bytes 2555912 | tf_op jit(solution)/shard_map/ppermute | solution.py:26
  23.3 37.5 %collective-permute-start.5 = (f32[2,8,104,128]{3,2,1,0:T(8,128)S(1)}, f32[2,8,104,128]{3,2,1,0:T(8,128)S(1)}, u32[]{:S(2)}, u32[]{:S(2)}) collective-permute-start(f32[2,8,104,128]{3,2,1,0:T(8,128)S(1)} %pad_maximum_fusion.refs_5_.refs_13_), channel_id=1, source_target_pairs={{0,8},{1,9},{2,10},{3,11},{4,12},{5,13},{6,14},{7,15},{8,0},{9,1},... | collective-permute-start | bytes 2555912 | tf_op jit(solution)/shard_map/ppermute | solution.py:26
  23.8 37.3 %collective-permute-start.4 = (f32[2,8,104,128]{3,2,1,0:T(8,128)S(1)}, f32[2,8,104,128]{3,2,1,0:T(8,128)S(1)}, u32[]{:S(2)}, u32[]{:S(2)}) collective-permute-start(f32[2,8,104,128]{3,2,1,0:T(8,128)S(1)} %pad_maximum_fusion.refs_5_.refs_13_), channel_id=1, source_target_pairs={{0,4},{1,5},{2,6},{3,7},{4,0},{5,1},{6,2},{7,3},{8,12},{9,13},{10,... | collective-permute-start | bytes 2555912 | tf_op jit(solution)/shard_map/ppermute | solution.py:26
  26.0 19.6 %collective-permute-start.3 = (s32[2,16,24,128]{3,2,1,0:T(8,128)S(1)}, s32[2,16,24,128]{3,2,1,0:T(8,128)S(1)}, u32[]{:S(2)}, u32[]{:S(2)}) collective-permute-start(s32[2,16,24,128]{3,2,1,0:T(8,128)S(1)} %pad_add_fusion.refs_0_), channel_id=1, source_target_pairs={{0,48},{1,49},{2,50},{3,51},{4,52},{5,53},{6,54},{7,55},{8,56},{9,... | collective-permute-start | bytes 1179656 | tf_op jit(solution)/shard_map/ppermute | solution.py:26
  29.9 15.8 %collective-permute-start.2 = (s32[2,16,24,128]{3,2,1,0:T(8,128)S(1)}, s32[2,16,24,128]{3,2,1,0:T(8,128)S(1)}, u32[]{:S(2)}, u32[]{:S(2)}) collective-permute-start(s32[2,16,24,128]{3,2,1,0:T(8,128)S(1)} %pad_add_fusion.refs_0_), channel_id=1, source_target_pairs={{0,16},{1,17},{2,18},{3,19},{4,20},{5,21},{6,22},{7,23},{8,24},{9,... | collective-permute-start | bytes 1179656 | tf_op jit(solution)/shard_map/ppermute | solution.py:26
  45.7 17.9 %collective-permute-start.7 = (s32[2,16,24,128]{3,2,1,0:T(8,128)}, s32[2,16,24,128]{3,2,1,0:T(8,128)S(1)}, u32[]{:S(2)}, u32[]{:S(2)}) collective-permute-start(s32[2,16,24,128]{3,2,1,0:T(8,128)} %copy-done.5), channel_id=1, source_target_pairs={{0,32},{1,33},{2,34},{3,35},{4,36},{5,37},{6,38},{7,39},{8,40},{9,... | collective-permute-start | bytes 1179656 | tf_op jit(solution)/shard_map/ppermute | solution.py:26
  61.2 8.5 %collective-permute-start.8 = (f32[2,8,104,128]{3,2,1,0:T(8,128)S(1)}, f32[2,8,104,128]{3,2,1,0:T(8,128)S(1)}, u32[]{:S(2)}, u32[]{:S(2)}) collective-permute-start(f32[2,8,104,128]{3,2,1,0:T(8,128)S(1)} %pad_maximum_fusion.refs_5_.refs_13_), channel_id=1, source_target_pairs={{0,1},{1,0},{2,3},{3,2},{4,5},{5,4},{6,7},{7,6},{8,9},{9,8},{10,11... | collective-permute-start | bytes 2555912 | tf_op jit(solution)/shard_map/ppermute | solution.py:26
  63.0 6.7 %collective-permute-start.9 = (f32[2,8,104,128]{3,2,1,0:T(8,128)S(1)}, f32[2,8,104,128]{3,2,1,0:T(8,128)S(1)}, u32[]{:S(2)}, u32[]{:S(2)}) collective-permute-start(f32[2,8,104,128]{3,2,1,0:T(8,128)S(1)} %collective-permute-done.4.refs_6_.refs_14_), channel_id=1, source_target_pairs={{0,1},{1,0},{2,3},{3,2},{4,5},{5,4},{6,7},{7,6},{8,9},{9,8},{10,11... | collective-permute-start | bytes 2555912 | tf_op jit(solution)/shard_map/ppermute | solution.py:26
  63.1 6.6 %collective-permute-start.10 = (f32[2,8,104,128]{3,2,1,0:T(8,128)S(1)}, f32[2,8,104,128]{3,2,1,0:T(8,128)S(1)}, u32[]{:S(2)}, u32[]{:S(2)}) collective-permute-start(f32[2,8,104,128]{3,2,1,0:T(8,128)S(1)} %collective-permute-done.5.refs_7_.refs_15_), channel_id=1, source_target_pairs={{0,1},{1,0},{2,3},{3,2},{4,5},{5,4},{6,7},{7,6},{8,9},{9,8},{10,11... | collective-permute-start | bytes 2555912 | tf_op jit(solution)/shard_map/ppermute | solution.py:26
  63.5 6.2 %collective-permute-start.11 = (f32[2,8,104,128]{3,2,1,0:T(8,128)S(1)}, f32[2,8,104,128]{3,2,1,0:T(8,128)S(1)}, u32[]{:S(2)}, u32[]{:S(2)}) collective-permute-start(f32[2,8,104,128]{3,2,1,0:T(8,128)S(1)} %collective-permute-done.6.refs_8_.refs_16_), channel_id=1, source_target_pairs={{0,1},{1,0},{2,3},{3,2},{4,5},{5,4},{6,7},{7,6},{8,9},{9,8},{10,11... | collective-permute-start | bytes 2555912 | tf_op jit(solution)/shard_map/ppermute | solution.py:26
  95.2 6.0 %collective-permute-start.15 = (f32[64,512]{1,0:T(8,128)S(1)}, f32[64,512]{1,0:T(8,128)S(1)}, u32[]{:S(2)}, u32[]{:S(2)}) collective-permute-start(f32[64,512]{1,0:T(8,128)S(1)} %get-tuple-element.54), channel_id=1, source_target_pairs={{0,12},{1,13},{2,14},{3,15},{4,8},{5,9},{6,10},{7,11},{8,4},{9,5},... | collective-permute-start | bytes 393224 | tf_op jit(solution)/shard_map/ppermute | solution.py:26
  97.0 7.8 %collective-permute-start.13 = (f32[64,512]{1,0:T(8,128)S(1)}, f32[64,512]{1,0:T(8,128)S(1)}, u32[]{:S(2)}, u32[]{:S(2)}) collective-permute-start(f32[64,512]{1,0:T(8,128)S(1)} %get-tuple-element.56), channel_id=1, source_target_pairs={{0,8},{1,9},{2,10},{3,11},{4,12},{5,13},{6,14},{7,15},{8,0},{9,1},... | collective-permute-start | bytes 393224 | tf_op jit(solution)/shard_map/ppermute | solution.py:26
  106.4 6.6 %collective-permute-start.16 = (f32[64,512]{1,0:T(8,128)S(1)}, f32[64,512]{1,0:T(8,128)S(1)}, u32[]{:S(2)}, u32[]{:S(2)}) collective-permute-start(f32[64,512]{1,0:T(8,128)S(1)} %fusion.1), channel_id=1, source_target_pairs={{0,2},{1,3},{2,0},{3,1},{4,6},{5,7},{6,4},{7,5},{8,10},{9,11},{10,... | collective-permute-start | bytes 393224 | tf_op jit(solution)/shard_map/ppermute | solution.py:26
  113.1 6.2 %collective-permute-start.21 = (f32[64,512]{1,0:T(8,128)S(1)}, f32[64,512]{1,0:T(8,128)S(1)}, u32[]{:S(2)}, u32[]{:S(2)}) collective-permute-start(f32[64,512]{1,0:T(8,128)S(1)} %add_add_fusion.3), channel_id=1, source_target_pairs={{0,48},{1,49},{2,50},{3,51},{4,52},{5,53},{6,54},{7,55},{8,56},{9,... | collective-permute-start | bytes 393224 | tf_op jit(solution)/shard_map/ppermute | solution.py:26
  117.0 5.4 %collective-permute-start.19 = (f32[64,512]{1,0:T(8,128)S(1)}, f32[64,512]{1,0:T(8,128)S(1)}, u32[]{:S(2)}, u32[]{:S(2)}) collective-permute-start(f32[64,512]{1,0:T(8,128)S(1)} %add_add_fusion.3), channel_id=1, source_target_pairs={{0,32},{1,33},{2,34},{3,35},{4,36},{5,37},{6,38},{7,39},{8,40},{9,... | collective-permute-start | bytes 393224 | tf_op jit(solution)/shard_map/ppermute | solution.py:26
  129.9 7.4 %collective-permute-start.25 = (f32[256,512]{1,0:T(8,128)S(1)}, f32[256,512]{1,0:T(8,128)S(1)}, u32[]{:S(2)}, u32[]{:S(2)}) collective-permute-start(f32[256,512]{1,0:T(8,128)S(1)} %pad_maximum_fusion.1.refs_21_.near_ref), channel_id=1, source_target_pairs={{0,1},{1,0},{2,3},{3,2},{4,5},{5,4},{6,7},{7,6},{8,9},{9,8},{10,11... | collective-permute-start | bytes 1572872 | tf_op jit(solution)/shard_map/ppermute | solution.py:26
  162.6 7.3 %collective-permute-start.29 = (f32[64,512]{1,0:T(8,128)S(1)}, f32[64,512]{1,0:T(8,128)S(1)}, u32[]{:S(2)}, u32[]{:S(2)}) collective-permute-start(f32[64,512]{1,0:T(8,128)S(1)} %get-tuple-element.51), channel_id=1, source_target_pairs={{0,12},{1,13},{2,14},{3,15},{4,8},{5,9},{6,10},{7,11},{8,4},{9,5},... | collective-permute-start | bytes 393224 | tf_op jit(solution)/shard_map/ppermute | solution.py:26
  164.4 5.5 %collective-permute-start.28 = (f32[64,512]{1,0:T(8,128)S(1)}, f32[64,512]{1,0:T(8,128)S(1)}, u32[]{:S(2)}, u32[]{:S(2)}) collective-permute-start(f32[64,512]{1,0:T(8,128)S(1)} %get-tuple-element.52), channel_id=1, source_target_pairs={{0,4},{1,5},{2,6},{3,7},{4,0},{5,1},{6,2},{7,3},{8,12},{9,13},{10,... | collective-permute-start | bytes 393224 | tf_op jit(solution)/shard_map/ppermute | solution.py:26
  164.4 7.9 %collective-permute-start.27 = (f32[64,512]{1,0:T(8,128)S(1)}, f32[64,512]{1,0:T(8,128)S(1)}, u32[]{:S(2)}, u32[]{:S(2)}) collective-permute-start(f32[64,512]{1,0:T(8,128)S(1)} %get-tuple-element.53), channel_id=1, source_target_pairs={{0,8},{1,9},{2,10},{3,11},{4,12},{5,13},{6,14},{7,15},{8,0},{9,1},... | collective-permute-start | bytes 393224 | tf_op jit(solution)/shard_map/ppermute | solution.py:26
  174.2 6.3 %collective-permute-start.30 = (f32[64,512]{1,0:T(8,128)S(1)}, f32[64,512]{1,0:T(8,128)S(1)}, u32[]{:S(2)}, u32[]{:S(2)}) collective-permute-start(f32[64,512]{1,0:T(8,128)S(1)} %fusion), channel_id=1, source_target_pairs={{0,2},{1,3},{2,0},{3,1},{4,6},{5,7},{6,4},{7,5},{8,10},{9,11},{10,... | collective-permute-start | bytes 393224 | tf_op jit(solution)/shard_map/ppermute | solution.py:26
  195.6 7.4 %collective-permute-start.39 = (f32[256,512]{1,0:T(8,128)S(1)}, f32[256,512]{1,0:T(8,128)S(1)}, u32[]{:S(2)}, u32[]{:S(2)}) collective-permute-start(f32[256,512]{1,0:T(8,128)S(1)} %pad_maximum_fusion.2.near_ref), channel_id=1, source_target_pairs={{0,1},{1,0},{2,3},{3,2},{4,5},{5,4},{6,7},{7,6},{8,9},{9,8},{10,11... | collective-permute-start | bytes 1572872 | tf_op jit(solution)/shard_map/ppermute | solution.py:26
  (33 other events, 186.0 us)

commit v4 on v3

--- a/solution.py
+++ b/solution.py
@@ -189,8 +189,8 @@
         counts = []
         for half in range(2):
             limit = (half * 128 + lane + 1) * 128
-            count = jnp.zeros((256, 128), I32)
-            for step in (64, 32, 16, 8, 4, 2, 1, 1):
+            count = jnp.where(code[:, spot(63) : spot(63) + 1] < limit, 64, 0)
+            for step in (32, 16, 8, 4, 2, 1, 1):
                 below = lanes(code, spot(count + (step - 1))) < limit
                 count = jnp.where(below, count + step, count)
             counts.append(count)
@@ -437,7 +437,7 @@
     mine, pieces = first(weights, codes, tile_map, codebooks)
     pieces = lax.all_to_all(pieces, "col", 0, 0, tiled=True)
     pair = pair_up(mine)
-    pieces, pair = hold(pieces, pair)
+    pieces, pair, where = hold(pieces, pair, where)
 
     around = over_x(pair)
     pieces = jnp.stack([pieces, swap(pieces, dyl=1)])

time: 208 us -> 207 us (level)
  no operation moved by 1% of the time
where the time goes in v4:
time: 207 us; the launch traced here: 206 us
  Pallas kernels  80.3 us (39%)
  starting transfers between devices  65.3 us (32%)
  waiting for transfers between devices  51.6 us (25%)
  local copies, waits for them, and re-layouts  4.85 us (2%)
  other arithmetic  4.22 us (2%)
    ppermute x40, starting transfers between devices, swap(): return lax.ppermute(v, BOTH, partners(dx, dyh, dcore, dyl, dz))  60 us
    ppermute x40, waiting for transfers between devices, swap(): return lax.ppermute(v, BOTH, partners(dx, dyh, dcore, dyl, dz))  48.5 us
    pallas_call x2, Pallas kernels, step(): pl.pallas_call(kernel, out_shape=[half, half], grid=(5,), in_specs=[in_sm...  40.9 us
    pallas_call x3, Pallas kernels, sort_codes(): pl.pallas_call(sort_kernel, out_shape=jax.ShapeDtypeStruct((2 * many, 264...  19.7 us
    pallas_call x1, Pallas kernels, split_hessian(): pl.pallas_call(split_kernel, out_shape=jax.ShapeDtypeStruct((8, 512, 1024...  10.5 us
    pallas_call x2, Pallas kernels, update(): pl.pallas_call(update_kernel, out_shape=jax.ShapeDtypeStruct((512, 2, 256...  6.55 us
    all_to_all x1, starting transfers between devices, per_device(): pieces = lax.all_to_all(pieces, 'col', 0, 0, tiled=True)  5.27 us
    unnamed x32, local copies, waits for them, and re-layouts  4.79 us
  transfers between devices with their start and end apart: 41, of which 29 were waited for; matrix products, arithmetic and copies ran while one was open for 1% of the time, Pallas kernels for 16%

profile of v4, /device:TPU:1, one launch (start us, length us, event | category | flops | bytes accessed | tf_op | source)
XLA Modules:
  0.0 206.4 jit_solution(7379909121596803596)
XLA Ops:
  0.0 2.6 %shard_map.55 = (f32[8,104,128]{2,1,0:T(8,128)}, s32[16,24,128]{2,1,0:T(8,128)}) custom-call(s32[2,8]{1,0:T(2,128)} %tile_ref.1, bf16[32,2048]{1,0:T(8,128)(2,1)} %weights_ref.1, s32[32,1024]{1,0:T(8,128)} %codes_ref.1, f32[512,2,256]{2,1,0:T(2,128)} %books_ref.3), custom_call_target="tpu_custom_call" | custom-call | tf_op jit(solution)/shard_map/pallas_call | solution.py:121
  2.6 3.7 %collective-permute-start = (f32[8,104,128]{2,1,0:T(8,128)}, f32[8,104,128]{2,1,0:T(8,128)S(1)}, u32[]{:S(2)}, u32[]{:S(2)}) collective-permute-start(f32[8,104,128]{2,1,0:T(8,128)} %get-tuple-element.30), channel_id=1, source_target_pairs={{0,2},{1,3},{2,0},{3,1},{4,6},{5,7},{6,4},{7,5},{8,10},{9,11},{10,... | collective-permute-start | bytes 1277960 | tf_op jit(solution)/shard_map/ppermute | solution.py:26
  6.3 5.3 %all-to-all-start = ((s32[16,24,128]{2,1,0:T(8,128)}), s32[16,24,128]{2,1,0:T(8,128)S(1)}, u32[]{:S(2)}, u32[]{:S(2)}) async-start(s32[16,24,128]{2,1,0:T(8,128)} %get-tuple-element.29), calls=%async_computation | async-start | bytes 393216 | tf_op jit(solution)/shard_map/all_to_all | solution.py:438
  12.2 3.6 %collective-permute-done = f32[8,104,128]{2,1,0:T(8,128)S(1)} collective-permute-done((f32[8,104,128]{2,1,0:T(8,128)}, f32[8,104,128]{2,1,0:T(8,128)S(1)}, u32[]{:S(2)}, u32[]{:S(2)}) %collective-permute-start) | collective-permute-done | bytes 426016 | tf_op jit(solution)/shard_map/ppermute | solution.py:26
  16.9 3.0 %all-to-all-done = s32[16,24,128]{2,1,0:T(8,128)S(1)} async-done(((s32[16,24,128]{2,1,0:T(8,128)}), s32[16,24,128]{2,1,0:T(8,128)S(1)}, u32[]{:S(2)}, u32[]{:S(2)}) %all-to-all-start) | async-done | bytes 196640 | tf_op jit(solution)/shard_map/all_to_all | solution.py:438
  26.0 3.8 %collective-permute-start.3 = (s32[2,16,24,128]{3,2,1,0:T(8,128)S(1)}, s32[2,16,24,128]{3,2,1,0:T(8,128)S(1)}, u32[]{:S(2)}, u32[]{:S(2)}) collective-permute-start(s32[2,16,24,128]{3,2,1,0:T(8,128)S(1)} %pad_add_fusion.refs_0_), channel_id=1, source_target_pairs={{0,48},{1,49},{2,50},{3,51},{4,52},{5,53},{6,54},{7,55},{8,56},{9,... | collective-permute-start | bytes 1179656 | tf_op jit(solution)/shard_map/ppermute | solution.py:26
  29.9 10.5 %shard_map.56.refs_3_.refs_4_ = bf16[8,512,1024]{2,1,0:T(8,128)(2,1)} custom-call(s32[3]{0:T(128)} %pad_add_fusion.1.where_ref, f32[16384,128]{1,0:T(8,128)} %bitcast.12), custom_call_target="tpu_custom_call" | custom-call | flops 8999999488 | bytes 20971520 | tf_op jit(solution)/shard_map/pallas_call | solution.py:220
  40.4 5.3 %shard_map.57.refs_0_ = s32[2,264,128]{2,1,0:T(8,128)} custom-call(s32[2,16,24,128]{3,2,1,0:T(8,128)} %copy-done.5), custom_call_target="tpu_custom_call" | custom-call | flops 5000000000 | bytes 1048576 | tf_op jit(solution)/shard_map/pallas_call | solution.py:199
  47.0 9.2 %shard_map.58.refs_1_ = s32[4,264,128]{2,1,0:T(8,128)} custom-call(s32[2,16,24,128]{3,2,1,0:T(8,128)} %copy-done.15, s32[2,16,24,128]{3,2,1,0:T(8,128)} %copy-done.14), custom_call_target="tpu_custom_call" | custom-call | flops 10000000000 | bytes 2097152 | tf_op jit(solution)/shard_map/pallas_call | solution.py:199
  56.2 4.0 %collective-permute-done.6.refs_8_.refs_16_ = f32[2,8,104,128]{3,2,1,0:T(8,128)S(1)} collective-permute-done((f32[2,8,104,128]{3,2,1,0:T(8,128)S(1)}, f32[2,8,104,128]{3,2,1,0:T(8,128)S(1)}, u32[]{:S(2)}, u32[]{:S(2)}) %collective-permute-start.6) | collective-permute-done | bytes 852000 | tf_op jit(solution)/shard_map/ppermute | solution.py:26
  63.8 5.3 %shard_map.59.refs_2_ = s32[2,264,128]{2,1,0:T(8,128)} custom-call(s32[2,16,24,128]{3,2,1,0:T(8,128)} %copy-done.13), custom_call_target="tpu_custom_call" | custom-call | flops 5000000000 | bytes 1048576 | tf_op jit(solution)/shard_map/pallas_call | solution.py:199
  71.5 19.7 %shard_map.60 = (f32[256,512]{1,0:T(8,128)}, f32[256,512]{1,0:T(8,128)}) custom-call(s32[3]{0:T(128)} %pad_add_fusion.1.where_ref, s32[2,264,128]{2,1,0:T(8,128)} %shard_map.57.refs_0_, s32[4,264,128]{2,1,0:T(8,128)} %shard_map.58.refs_1_, s32[2,264,128]{2,1,0:T(8,128)} %shard_map.59.refs_2_, bf16[8,512,1024]{2,1,0:T(8,128)(2,1)} %shard_map.56.refs_3_.refs_4_, ...), custom_call_target="tpu_custom_call" | custom-call | flops 17999998976 | bytes 16777216 | tf_op jit(solution)/shard_map/pallas_call | solution.py:356
  100.8 3.4 %collective-permute-done.13 = f32[64,512]{1,0:T(8,128)S(1)} collective-permute-done((f32[64,512]{1,0:T(8,128)S(1)}, f32[64,512]{1,0:T(8,128)S(1)}, u32[]{:S(2)}, u32[]{:S(2)}) %collective-permute-start.13) | collective-permute-done | bytes 131104 | tf_op jit(solution)/shard_map/ppermute | solution.py:26
  105.8 2.4 %collective-permute-start.16 = (f32[64,512]{1,0:T(8,128)S(1)}, f32[64,512]{1,0:T(8,128)S(1)}, u32[]{:S(2)}, u32[]{:S(2)}) collective-permute-start(f32[64,512]{1,0:T(8,128)S(1)} %fusion.1), channel_id=1, source_target_pairs={{0,2},{1,3},{2,0},{3,1},{4,6},{5,7},{6,4},{7,5},{8,10},{9,11},{10,... | collective-permute-start | bytes 393224 | tf_op jit(solution)/shard_map/ppermute | solution.py:26
  109.4 3.1 %collective-permute-done.16 = f32[64,512]{1,0:T(8,128)S(1)} collective-permute-done((f32[64,512]{1,0:T(8,128)S(1)}, f32[64,512]{1,0:T(8,128)S(1)}, u32[]{:S(2)}, u32[]{:S(2)}) %collective-permute-start.16) | collective-permute-done | bytes 131104 | tf_op jit(solution)/shard_map/ppermute | solution.py:26
  112.5 3.8 %collective-permute-start.21 = (f32[64,512]{1,0:T(8,128)S(1)}, f32[64,512]{1,0:T(8,128)S(1)}, u32[]{:S(2)}, u32[]{:S(2)}) collective-permute-start(f32[64,512]{1,0:T(8,128)S(1)} %add_add_fusion.3), channel_id=1, source_target_pairs={{0,48},{1,49},{2,50},{3,51},{4,52},{5,53},{6,54},{7,55},{8,56},{9,... | collective-permute-start | bytes 393224 | tf_op jit(solution)/shard_map/ppermute | solution.py:26
  129.3 5.9 %collective-permute-start.25 = (f32[256,512]{1,0:T(8,128)S(1)}, f32[256,512]{1,0:T(8,128)S(1)}, u32[]{:S(2)}, u32[]{:S(2)}) collective-permute-start(f32[256,512]{1,0:T(8,128)S(1)} %pad_maximum_fusion.1.refs_21_.near_ref), channel_id=1, source_target_pairs={{0,1},{1,0},{2,3},{3,2},{4,5},{5,4},{6,7},{7,6},{8,9},{9,8},{10,11... | collective-permute-start | bytes 1572872 | tf_op jit(solution)/shard_map/ppermute | solution.py:26
  137.5 21.2 %shard_map.61 = (f32[256,512]{1,0:T(8,128)}, f32[256,512]{1,0:T(8,128)}) custom-call(s32[3]{0:T(128)} %pad_add_fusion.1.where_ref, s32[2,264,128]{2,1,0:T(8,128)} %shard_map.57.refs_0_, s32[4,264,128]{2,1,0:T(8,128)} %shard_map.58.refs_1_, s32[2,264,128]{2,1,0:T(8,128)} %shard_map.59.refs_2_, bf16[8,512,1024]{2,1,0:T(8,128)(2,1)} %shard_map.56.refs_3_.refs_4_, ...), custom_call_target="tpu_custom_call" | custom-call | flops 17999998976 | bytes 16777216 | tf_op jit(solution)/shard_map/pallas_call | solution.py:356
  166.0 3.3 %shard_map.62.books_ref = f32[512,2,256]{2,1,0:T(2,128)} custom-call(s32[3]{0:T(128)} %pad_add_fusion.1.where_ref, f32[512,2,256]{2,1,0:T(2,128)} %books_ref.3, f32[256,512]{1,0:T(8,128)} %copy-done, f32[256,512]{1,0:T(8,128)} %copy-done.3), custom_call_target="tpu_custom_call" | custom-call | tf_op jit(solution)/shard_map/pallas_call | solution.py:396
  169.3 2.4 %collective-permute-done.27 = f32[64,512]{1,0:T(8,128)S(1)} collective-permute-done((f32[64,512]{1,0:T(8,128)S(1)}, f32[64,512]{1,0:T(8,128)S(1)}, u32[]{:S(2)}, u32[]{:S(2)}) %collective-permute-start.27) | collective-permute-done | bytes 131104 | tf_op jit(solution)/shard_map/ppermute | solution.py:26
  177.4 2.5 %collective-permute-done.30 = f32[64,512]{1,0:T(8,128)S(1)} collective-permute-done((f32[64,512]{1,0:T(8,128)S(1)}, f32[64,512]{1,0:T(8,128)S(1)}, u32[]{:S(2)}, u32[]{:S(2)}) %collective-permute-start.30) | collective-permute-done | bytes 131104 | tf_op jit(solution)/shard_map/ppermute | solution.py:26
  180.0 2.4 %collective-permute-start.35 = (f32[64,512]{1,0:T(8,128)S(1)}, f32[64,512]{1,0:T(8,128)S(1)}, u32[]{:S(2)}, u32[]{:S(2)}) collective-permute-start(f32[64,512]{1,0:T(8,128)S(1)} %add_add_fusion.1), channel_id=1, source_target_pairs={{0,48},{1,49},{2,50},{3,51},{4,52},{5,53},{6,54},{7,55},{8,56},{9,... | collective-permute-start | bytes 393224 | tf_op jit(solution)/shard_map/ppermute | solution.py:26
  195.0 5.8 %collective-permute-start.39 = (f32[256,512]{1,0:T(8,128)S(1)}, f32[256,512]{1,0:T(8,128)S(1)}, u32[]{:S(2)}, u32[]{:S(2)}) collective-permute-start(f32[256,512]{1,0:T(8,128)S(1)} %pad_maximum_fusion.2.near_ref), channel_id=1, source_target_pairs={{0,1},{1,0},{2,3},{3,2},{4,5},{5,4},{6,7},{7,6},{8,9},{9,8},{10,11... | collective-permute-start | bytes 1572872 | tf_op jit(solution)/shard_map/ppermute | solution.py:26
  203.2 3.2 %shard_map.63 = f32[512,2,256]{2,1,0:T(2,128)} custom-call(s32[3]{0:T(128)} %pad_add_fusion.1.where_ref, f32[512,2,256]{2,1,0:T(2,128)} %shard_map.62.books_ref, f32[256,512]{1,0:T(8,128)} %copy-done.1, f32[256,512]{1,0:T(8,128)} %copy-done.4), custom_call_target="tpu_custom_call" | custom-call | tf_op jit(solution)/shard_map/pallas_call | solution.py:396
  (114 shorter events, 70.7 us)
Async XLA Ops:
  2.6 13.2 %collective-permute-start = (f32[8,104,128]{2,1,0:T(8,128)}, f32[8,104,128]{2,1,0:T(8,128)S(1)}, u32[]{:S(2)}, u32[]{:S(2)}) collective-permute-start(f32[8,104,128]{2,1,0:T(8,128)} %get-tuple-element.30), channel_id=1, source_target_pairs={{0,2},{1,3},{2,0},{3,1},{4,6},{5,7},{6,4},{7,5},{8,10},{9,11},{10,... | collective-permute-start | bytes 1277960 | tf_op jit(solution)/shard_map/ppermute | solution.py:26
  6.3 13.6 %all-to-all-start = ((s32[16,24,128]{2,1,0:T(8,128)}), s32[16,24,128]{2,1,0:T(8,128)S(1)}, u32[]{:S(2)}, u32[]{:S(2)}) async-start(s32[16,24,128]{2,1,0:T(8,128)} %get-tuple-element.29), calls=%async_computation | async-start | bytes 393216 | tf_op jit(solution)/shard_map/all_to_all | solution.py:438
  19.9 6.1 %collective-permute-start.1 = (s32[16,24,128]{2,1,0:T(8,128)S(1)}, s32[16,24,128]{2,1,0:T(8,128)S(1)}, u32[]{:S(2)}, u32[]{:S(2)}) collective-permute-start(s32[16,24,128]{2,1,0:T(8,128)S(1)} %all-to-all-done), channel_id=1, source_target_pairs={{0,64},{1,65},{2,66},{3,67},{4,68},{5,69},{6,70},{7,71},{8,72},{9,... | collective-permute-start | bytes 589832 | tf_op jit(solution)/shard_map/ppermute | solution.py:26
  21.0 39.3 %collective-permute-start.6 = (f32[2,8,104,128]{3,2,1,0:T(8,128)S(1)}, f32[2,8,104,128]{3,2,1,0:T(8,128)S(1)}, u32[]{:S(2)}, u32[]{:S(2)}) collective-permute-start(f32[2,8,104,128]{3,2,1,0:T(8,128)S(1)} %pad_maximum_fusion.refs_5_.refs_13_), channel_id=1, source_target_pairs={{0,12},{1,13},{2,14},{3,15},{4,8},{5,9},{6,10},{7,11},{8,4},{9,5},... | collective-permute-start | bytes 2555912 | tf_op jit(solution)/shard_map/ppermute | solution.py:26
  22.7 37.5 %collective-permute-start.5 = (f32[2,8,104,128]{3,2,1,0:T(8,128)S(1)}, f32[2,8,104,128]{3,2,1,0:T(8,128)S(1)}, u32[]{:S(2)}, u32[]{:S(2)}) collective-permute-start(f32[2,8,104,128]{3,2,1,0:T(8,128)S(1)} %pad_maximum_fusion.refs_5_.refs_13_), channel_id=1, source_target_pairs={{0,8},{1,9},{2,10},{3,11},{4,12},{5,13},{6,14},{7,15},{8,0},{9,1},... | collective-permute-start | bytes 2555912 | tf_op jit(solution)/shard_map/ppermute | solution.py:26
  23.2 37.3 %collective-permute-start.4 = (f32[2,8,104,128]{3,2,1,0:T(8,128)S(1)}, f32[2,8,104,128]{3,2,1,0:T(8,128)S(1)}, u32[]{:S(2)}, u32[]{:S(2)}) collective-permute-start(f32[2,8,104,128]{3,2,1,0:T(8,128)S(1)} %pad_maximum_fusion.refs_5_.refs_13_), channel_id=1, source_target_pairs={{0,4},{1,5},{2,6},{3,7},{4,0},{5,1},{6,2},{7,3},{8,12},{9,13},{10,... | collective-permute-start | bytes 2555912 | tf_op jit(solution)/shard_map/ppermute | solution.py:26
  26.0 19.6 %collective-permute-start.3 = (s32[2,16,24,128]{3,2,1,0:T(8,128)S(1)}, s32[2,16,24,128]{3,2,1,0:T(8,128)S(1)}, u32[]{:S(2)}, u32[]{:S(2)}) collective-permute-start(s32[2,16,24,128]{3,2,1,0:T(8,128)S(1)} %pad_add_fusion.refs_0_), channel_id=1, source_target_pairs={{0,48},{1,49},{2,50},{3,51},{4,52},{5,53},{6,54},{7,55},{8,56},{9,... | collective-permute-start | bytes 1179656 | tf_op jit(solution)/shard_map/ppermute | solution.py:26
  29.9 15.8 %collective-permute-start.2 = (s32[2,16,24,128]{3,2,1,0:T(8,128)S(1)}, s32[2,16,24,128]{3,2,1,0:T(8,128)S(1)}, u32[]{:S(2)}, u32[]{:S(2)}) collective-permute-start(s32[2,16,24,128]{3,2,1,0:T(8,128)S(1)} %pad_add_fusion.refs_0_), channel_id=1, source_target_pairs={{0,16},{1,17},{2,18},{3,19},{4,20},{5,21},{6,22},{7,23},{8,24},{9,... | collective-permute-start | bytes 1179656 | tf_op jit(solution)/shard_map/ppermute | solution.py:26
  45.7 17.3 %collective-permute-start.7 = (s32[2,16,24,128]{3,2,1,0:T(8,128)}, s32[2,16,24,128]{3,2,1,0:T(8,128)S(1)}, u32[]{:S(2)}, u32[]{:S(2)}) collective-permute-start(s32[2,16,24,128]{3,2,1,0:T(8,128)} %copy-done.5), channel_id=1, source_target_pairs={{0,32},{1,33},{2,34},{3,35},{4,36},{5,37},{6,38},{7,39},{8,40},{9,... | collective-permute-start | bytes 1179656 | tf_op jit(solution)/shard_map/ppermute | solution.py:26
  60.6 8.5 %collective-permute-start.8 = (f32[2,8,104,128]{3,2,1,0:T(8,128)S(1)}, f32[2,8,104,128]{3,2,1,0:T(8,128)S(1)}, u32[]{:S(2)}, u32[]{:S(2)}) collective-permute-start(f32[2,8,104,128]{3,2,1,0:T(8,128)S(1)} %pad_maximum_fusion.refs_5_.refs_13_), channel_id=1, source_target_pairs={{0,1},{1,0},{2,3},{3,2},{4,5},{5,4},{6,7},{7,6},{8,9},{9,8},{10,11... | collective-permute-start | bytes 2555912 | tf_op jit(solution)/shard_map/ppermute | solution.py:26
  62.4 6.7 %collective-permute-start.9 = (f32[2,8,104,128]{3,2,1,0:T(8,128)S(1)}, f32[2,8,104,128]{3,2,1,0:T(8,128)S(1)}, u32[]{:S(2)}, u32[]{:S(2)}) collective-permute-start(f32[2,8,104,128]{3,2,1,0:T(8,128)S(1)} %collective-permute-done.4.refs_6_.refs_14_), channel_id=1, source_target_pairs={{0,1},{1,0},{2,3},{3,2},{4,5},{5,4},{6,7},{7,6},{8,9},{9,8},{10,11... | collective-permute-start | bytes 2555912 | tf_op jit(solution)/shard_map/ppermute | solution.py:26
  62.5 6.6 %collective-permute-start.10 = (f32[2,8,104,128]{3,2,1,0:T(8,128)S(1)}, f32[2,8,104,128]{3,2,1,0:T(8,128)S(1)}, u32[]{:S(2)}, u32[]{:S(2)}) collective-permute-start(f32[2,8,104,128]{3,2,1,0:T(8,128)S(1)} %collective-permute-done.5.refs_7_.refs_15_), channel_id=1, source_target_pairs={{0,1},{1,0},{2,3},{3,2},{4,5},{5,4},{6,7},{7,6},{8,9},{9,8},{10,11... | collective-permute-start | bytes 2555912 | tf_op jit(solution)/shard_map/ppermute | solution.py:26
  62.9 6.2 %collective-permute-start.11 = (f32[2,8,104,128]{3,2,1,0:T(8,128)S(1)}, f32[2,8,104,128]{3,2,1,0:T(8,128)S(1)}, u32[]{:S(2)}, u32[]{:S(2)}) collective-permute-start(f32[2,8,104,128]{3,2,1,0:T(8,128)S(1)} %collective-permute-done.6.refs_8_.refs_16_), channel_id=1, source_target_pairs={{0,1},{1,0},{2,3},{3,2},{4,5},{5,4},{6,7},{7,6},{8,9},{9,8},{10,11... | collective-permute-start | bytes 2555912 | tf_op jit(solution)/shard_map/ppermute | solution.py:26
  94.6 6.0 %collective-permute-start.15 = (f32[64,512]{1,0:T(8,128)S(1)}, f32[64,512]{1,0:T(8,128)S(1)}, u32[]{:S(2)}, u32[]{:S(2)}) collective-permute-start(f32[64,512]{1,0:T(8,128)S(1)} %get-tuple-element.56), channel_id=1, source_target_pairs={{0,12},{1,13},{2,14},{3,15},{4,8},{5,9},{6,10},{7,11},{8,4},{9,5},... | collective-permute-start | bytes 393224 | tf_op jit(solution)/shard_map/ppermute | solution.py:26
  96.5 7.8 %collective-permute-start.13 = (f32[64,512]{1,0:T(8,128)S(1)}, f32[64,512]{1,0:T(8,128)S(1)}, u32[]{:S(2)}, u32[]{:S(2)}) collective-permute-start(f32[64,512]{1,0:T(8,128)S(1)} %get-tuple-element.58), channel_id=1, source_target_pairs={{0,8},{1,9},{2,10},{3,11},{4,12},{5,13},{6,14},{7,15},{8,0},{9,1},... | collective-permute-start | bytes 393224 | tf_op jit(solution)/shard_map/ppermute | solution.py:26
  105.8 6.6 %collective-permute-start.16 = (f32[64,512]{1,0:T(8,128)S(1)}, f32[64,512]{1,0:T(8,128)S(1)}, u32[]{:S(2)}, u32[]{:S(2)}) collective-permute-start(f32[64,512]{1,0:T(8,128)S(1)} %fusion.1), channel_id=1, source_target_pairs={{0,2},{1,3},{2,0},{3,1},{4,6},{5,7},{6,4},{7,5},{8,10},{9,11},{10,... | collective-permute-start | bytes 393224 | tf_op jit(solution)/shard_map/ppermute | solution.py:26
  112.5 6.2 %collective-permute-start.21 = (f32[64,512]{1,0:T(8,128)S(1)}, f32[64,512]{1,0:T(8,128)S(1)}, u32[]{:S(2)}, u32[]{:S(2)}) collective-permute-start(f32[64,512]{1,0:T(8,128)S(1)} %add_add_fusion.3), channel_id=1, source_target_pairs={{0,48},{1,49},{2,50},{3,51},{4,52},{5,53},{6,54},{7,55},{8,56},{9,... | collective-permute-start | bytes 393224 | tf_op jit(solution)/shard_map/ppermute | solution.py:26
  116.4 5.4 %collective-permute-start.19 = (f32[64,512]{1,0:T(8,128)S(1)}, f32[64,512]{1,0:T(8,128)S(1)}, u32[]{:S(2)}, u32[]{:S(2)}) collective-permute-start(f32[64,512]{1,0:T(8,128)S(1)} %add_add_fusion.3), channel_id=1, source_target_pairs={{0,32},{1,33},{2,34},{3,35},{4,36},{5,37},{6,38},{7,39},{8,40},{9,... | collective-permute-start | bytes 393224 | tf_op jit(solution)/shard_map/ppermute | solution.py:26
  129.3 7.4 %collective-permute-start.25 = (f32[256,512]{1,0:T(8,128)S(1)}, f32[256,512]{1,0:T(8,128)S(1)}, u32[]{:S(2)}, u32[]{:S(2)}) collective-permute-start(f32[256,512]{1,0:T(8,128)S(1)} %pad_maximum_fusion.1.refs_21_.near_ref), channel_id=1, source_target_pairs={{0,1},{1,0},{2,3},{3,2},{4,5},{5,4},{6,7},{7,6},{8,9},{9,8},{10,11... | collective-permute-start | bytes 1572872 | tf_op jit(solution)/shard_map/ppermute | solution.py:26
  162.1 7.3 %collective-permute-start.29 = (f32[64,512]{1,0:T(8,128)S(1)}, f32[64,512]{1,0:T(8,128)S(1)}, u32[]{:S(2)}, u32[]{:S(2)}) collective-permute-start(f32[64,512]{1,0:T(8,128)S(1)} %get-tuple-element.53), channel_id=1, source_target_pairs={{0,12},{1,13},{2,14},{3,15},{4,8},{5,9},{6,10},{7,11},{8,4},{9,5},... | collective-permute-start | bytes 393224 | tf_op jit(solution)/shard_map/ppermute | solution.py:26
  163.8 5.5 %collective-permute-start.28 = (f32[64,512]{1,0:T(8,128)S(1)}, f32[64,512]{1,0:T(8,128)S(1)}, u32[]{:S(2)}, u32[]{:S(2)}) collective-permute-start(f32[64,512]{1,0:T(8,128)S(1)} %get-tuple-element.54), channel_id=1, source_target_pairs={{0,4},{1,5},{2,6},{3,7},{4,0},{5,1},{6,2},{7,3},{8,12},{9,13},{10,... | collective-permute-start | bytes 393224 | tf_op jit(solution)/shard_map/ppermute | solution.py:26
  163.8 7.9 %collective-permute-start.27 = (f32[64,512]{1,0:T(8,128)S(1)}, f32[64,512]{1,0:T(8,128)S(1)}, u32[]{:S(2)}, u32[]{:S(2)}) collective-permute-start(f32[64,512]{1,0:T(8,128)S(1)} %get-tuple-element.55), channel_id=1, source_target_pairs={{0,8},{1,9},{2,10},{3,11},{4,12},{5,13},{6,14},{7,15},{8,0},{9,1},... | collective-permute-start | bytes 393224 | tf_op jit(solution)/shard_map/ppermute | solution.py:26
  173.6 6.3 %collective-permute-start.30 = (f32[64,512]{1,0:T(8,128)S(1)}, f32[64,512]{1,0:T(8,128)S(1)}, u32[]{:S(2)}, u32[]{:S(2)}) collective-permute-start(f32[64,512]{1,0:T(8,128)S(1)} %fusion), channel_id=1, source_target_pairs={{0,2},{1,3},{2,0},{3,1},{4,6},{5,7},{6,4},{7,5},{8,10},{9,11},{10,... | collective-permute-start | bytes 393224 | tf_op jit(solution)/shard_map/ppermute | solution.py:26
  195.0 7.4 %collective-permute-start.39 = (f32[256,512]{1,0:T(8,128)S(1)}, f32[256,512]{1,0:T(8,128)S(1)}, u32[]{:S(2)}, u32[]{:S(2)}) collective-permute-start(f32[256,512]{1,0:T(8,128)S(1)} %pad_maximum_fusion.2.near_ref), channel_id=1, source_target_pairs={{0,1},{1,0},{2,3},{3,2},{4,5},{5,4},{6,7},{7,6},{8,9},{9,8},{10,11... | collective-permute-start | bytes 1572872 | tf_op jit(solution)/shard_map/ppermute | solution.py:26
  (33 other events, 185.4 us)
